TPU v7x, 32 devices: a whole 2x2x4 slice. The times are simulated.
32 devices in a mesh: batch: 8 (over y, x, core), rows: 4 (over z).
Axes of the slice: x: 2, y: 2, z: 4, core: 2. Of those that a mesh axis runs over, the one named last changes fastest.
Arguments:
- patches: bfloat16 [16, 32, 32, 384], P('batch', 'rows'), may hold values from -6 to 6
- cotangent: bfloat16 [16, 32, 32, 384], P('batch', 'rows'), may hold values from -6 to 6
- heights: int32 [16], P('batch'), may hold values from 8 to 32, as said below
- widths: int32 [16], P('batch'), may hold values from 8 to 32, as said below
- qkv_weight: float32 [384, 1152], P(None, 'rows'), may hold values from -0.4375 to 0.4375
- qkv_moment: float32 [384, 1152], P(None, 'rows'), may hold values from -512 to 512
- proj_weight: float32 [384, 384], P(None, 'rows'), may hold values from -0.625 to 0.625
- proj_moment: float32 [384, 384], P(None, 'rows'), may hold values from -512 to 512
- expand_weight: float32 [384, 1536], P(None, 'rows'), may hold values from -0.3125 to 0.3125
- expand_moment: float32 [384, 1536], P(None, 'rows'), may hold values from -512 to 512
- shrink_weight: float32 [1536, 384], P('rows'), may hold values from -0.15625 to 0.15625
- shrink_moment: float32 [1536, 384], P('rows'), may hold values from -512 to 512
- norm_gains: float32 [2, 384], replicated, may hold values from 0.5 to 1.5
- gains_moment: float32 [2, 384], P(None, 'rows'), may hold values from -512 to 512
- all_biases: float32 [4224], replicated, may hold values from -1 to 1
- biases_moment: float32 [4224], P('rows'), may hold values from -512 to 512
- frequencies: float32 [2, 192], replicated, may hold values from -0.5 to 0.5
- freq_moment: float32 [2, 192], P(None, 'rows'), may hold values from -4096 to 4096
Outputs:
- block_out: bfloat16 [16, 32, 32, 384], P('batch', 'rows')
- patch_grad: float32 [16, 32, 32, 384], P('batch', 'rows')
- qkv_moment_new: float32 [384, 1152], P(None, 'rows')
- qkv_weight_new: float32 [384, 1152], P(None, 'rows')
- proj_moment_new: float32 [384, 384], P(None, 'rows')
- proj_weight_new: float32 [384, 384], P(None, 'rows')
- expand_moment_new: float32 [384, 1536], P(None, 'rows')
- expand_weight_new: float32 [384, 1536], P(None, 'rows')
- shrink_moment_new: float32 [1536, 384], P('rows')
- shrink_weight_new: float32 [1536, 384], P('rows')
- gains_moment_new: float32 [2, 384], P(None, 'rows')
- norm_gains_new: float32 [2, 384], P(None, 'rows')
- biases_moment_new: float32 [4224], P('rows')
- all_biases_new: float32 [4224], P('rows')
- freq_moment_new: float32 [2, 192], P(None, 'rows')
- frequencies_new: float32 [2, 192], P(None, 'rows')
Inputs may be any that keep to these rules, and one draw needn't show every extreme that they name: `heights`: in each block of 2 images that one device index of batch holds, one image, drawn from the seed, has 32 rows and 32 columns. `widths`: in each block of 2 images that one device index of batch holds, one image, drawn from the seed, has 32 rows and 32 columns.
All inputs are finite; a program needn't handle non-finite values.
Results may differ from a plain program's by a relative error of at most 0.01.
The roundings to bfloat16 on the way count: a program that leaves them out, or rounds other values in their place, can miss the bound.
Values may be sent and summed in bfloat16 or wider, within the bound.
No kernel may reach another device: no remote copies, remote signals or barrier semaphores. Data moves between devices by JAX's collectives and lax.ppermute only.
A program may use at most 448 MiB of HBM per device.

v0:
```python
import math

import jax
import jax.numpy as jnp
from jax import lax
from jax.sharding import PartitionSpec as P

D = 384
H = 6
HD = 64
FF = 1536


highest = lax.Precision.HIGHEST
coeff_one = 3.4445
coeff_two = -4.775
coeff_three = 2.0315


def layer_norm(values, gain_row, shift_row):
    centered = values - jnp.mean(values, axis=-1, keepdims=True)
    variance = jnp.mean(centered * centered, axis=-1, keepdims=True)
    return centered * lax.rsqrt(variance + 1e-06) * gain_row + shift_row


def exact_gelu(values):
    return jax.nn.gelu(values, approximate=False)


def rotate_half(values, cosine, sine_part):
    half_dim = values.shape[-1] // 2
    first_half = values[..., :half_dim]
    second_half = values[..., half_dim:]
    return jnp.concatenate(
        [
            first_half * cosine - second_half * sine_part,
            second_half * cosine + first_half * sine_part,
        ],
        axis=-1,
    )


def turn_both(queries, keys_raw, frequencies, row_float, col_float):
    angles = (
        row_float[:, None] * frequencies[0][None, :] + col_float[:, None] * frequencies[1][None, :]
    )
    angles = angles.reshape(row_float.shape[0], H, HD // 2)
    cosine = jnp.cos(angles)
    sine_part = jnp.sin(angles)
    return (rotate_half(queries, cosine, sine_part), rotate_half(keys_raw, cosine, sine_part))


def head_slice(stacked, image_at, head_at):
    return lax.dynamic_slice(stacked, (image_at, 0, head_at * HD), (1, stacked.shape[1], HD))[0]


def heads_last(stacked, images):
    return (
        stacked.reshape(images, H, stacked.shape[1], HD)
        .transpose(0, 2, 1, 3)
        .reshape(images, stacked.shape[1], H * HD)
    )


def masked_scores(query_head, key_head, valid_keys, score_scale):
    scores = (
        jnp.einsum("sd,ld->sl", query_head, key_head, preferred_element_type=jnp.float32)
        * score_scale
    )
    return jnp.where(valid_keys[None, :], scores, -1000000000.0)


def local(
    patches,
    cotangent,
    heights,
    widths,
    qkv_weight,
    qkv_moment,
    proj_weight,
    proj_moment,
    expand_weight,
    expand_moment,
    shrink_weight,
    shrink_moment,
    norm_gains,
    gains_moment,
    all_biases,
    biases_moment,
    frequencies,
    freq_moment,
):
    images, band_rows, grid_w, width_d = patches.shape
    bands = lax.axis_size("rows")
    band_index = lax.axis_index("rows")
    grid_h = band_rows * bands
    tokens = band_rows * grid_w
    rows_all = images * tokens
    item_count = images * H
    score_scale = HD ** (-0.5)
    qkv16, proj16, expand16, shrink16 = (
        lax.all_gather(qkv_weight.astype(jnp.bfloat16), "rows", axis=1, tiled=True),
        lax.all_gather(proj_weight.astype(jnp.bfloat16), "rows", axis=1, tiled=True),
        lax.all_gather(expand_weight.astype(jnp.bfloat16), "rows", axis=1, tiled=True),
        lax.all_gather(shrink_weight.astype(jnp.bfloat16), "rows", axis=0, tiled=True),
    )
    shift_one = all_biases[0:D]
    shift_two = all_biases[D : 2 * D]
    qkv_bias = all_biases[2 * D : 5 * D]
    proj_bias = all_biases[5 * D : 6 * D]
    expand_bias = all_biases[6 * D : 6 * D + FF]
    shrink_bias = all_biases[6 * D + FF :]
    local_rows = band_index * band_rows + jnp.repeat(jnp.arange(band_rows, dtype=jnp.int32), grid_w)
    local_cols = jnp.tile(jnp.arange(grid_w, dtype=jnp.int32), band_rows)
    key_rows = jnp.repeat(jnp.arange(grid_h, dtype=jnp.int32), grid_w)
    key_cols = jnp.tile(jnp.arange(grid_w, dtype=jnp.int32), grid_h)
    query_valid = (local_rows[None, :] < heights[:, None]) & (local_cols[None, :] < widths[:, None])
    key_valid = (key_rows[None, :] < heights[:, None]) & (key_cols[None, :] < widths[:, None])
    valid_column = query_valid.reshape(rows_all, 1)
    row_float = local_rows.astype(jnp.float32)
    col_float = local_cols.astype(jnp.float32)
    flat_rows = patches.reshape(rows_all, D).astype(jnp.float32)
    normed, norm_back_one = jax.vjp(layer_norm, flat_rows, norm_gains[0], shift_one)
    normed16 = normed.astype(jnp.bfloat16)
    mixed_proj = jnp.dot(normed16, qkv16, preferred_element_type=jnp.float32) + qkv_bias
    queries = mixed_proj[:, :D].reshape(images, tokens, H, HD)
    keys_raw = mixed_proj[:, D : 2 * D].reshape(images, tokens, H, HD)
    values16 = mixed_proj[:, 2 * D :].astype(jnp.bfloat16).reshape(images, tokens, D)

    def rotate_here(query_part, key_part, freq_part):
        return turn_both(query_part, key_part, freq_part, row_float, col_float)

    (query_rot, key_rot), turn_back = jax.vjp(rotate_here, queries, keys_raw, frequencies)
    query16 = query_rot.astype(jnp.bfloat16).reshape(images, tokens, D)
    key16 = key_rot.astype(jnp.bfloat16).reshape(images, tokens, D)
    key_all, value_all = (
        lax.all_gather(key16, "rows", axis=1, tiled=True),
        lax.all_gather(values16, "rows", axis=1, tiled=True),
    )

    def attend_forward(item_index):
        image_at = item_index // H
        head_at = item_index % H
        query_head = head_slice(query16, image_at, head_at)
        key_head = head_slice(key_all, image_at, head_at)
        value_head = head_slice(value_all, image_at, head_at)
        valid_keys = lax.dynamic_index_in_dim(key_valid, image_at, 0, keepdims=False)
        scores = masked_scores(query_head, key_head, valid_keys, score_scale)
        row_peak = jnp.max(scores, axis=-1, keepdims=True)
        shifted = jnp.exp(scores - row_peak)
        row_total = jnp.sum(shifted, axis=-1, keepdims=True)
        attn_probs = (shifted / row_total).astype(jnp.bfloat16)
        head_out = jnp.einsum(
            "sl,ld->sd", attn_probs, value_head, preferred_element_type=jnp.float32
        )
        return (head_out.astype(jnp.bfloat16), (row_peak + jnp.log(row_total))[:, 0])

    head_outs, log_totals = lax.map(attend_forward, jnp.arange(item_count, dtype=jnp.int32))
    attended16 = heads_last(head_outs, images).reshape(rows_all, D)
    residual = (
        flat_rows + jnp.dot(attended16, proj16, preferred_element_type=jnp.float32) + proj_bias
    )
    normed_two, norm_back_two = jax.vjp(layer_norm, residual, norm_gains[1], shift_two)
    normed_two16 = normed_two.astype(jnp.bfloat16)
    hidden_pre = jnp.dot(normed_two16, expand16, preferred_element_type=jnp.float32) + expand_bias
    hidden_full, gelu_back = jax.vjp(exact_gelu, hidden_pre)
    hidden16 = hidden_full.astype(jnp.bfloat16)
    result = (
        residual + jnp.dot(hidden16, shrink16, preferred_element_type=jnp.float32) + shrink_bias
    )
    block_out = (
        (result * valid_column.astype(jnp.float32))
        .astype(jnp.bfloat16)
        .reshape(images, band_rows, grid_w, D)
    )
    grad16 = cotangent.reshape(rows_all, D) * valid_column.astype(jnp.bfloat16)
    grad_out = grad16.astype(jnp.float32)
    d_shrink = jnp.einsum("nf,nd->fd", hidden16, grad16, preferred_element_type=jnp.float32)
    d_shrink_bias = jnp.sum(grad_out, axis=0)
    d_hidden = jnp.einsum("nd,fd->nf", grad16, shrink16, preferred_element_type=jnp.float32)
    d_pre16 = gelu_back(d_hidden)[0].astype(jnp.bfloat16)
    d_expand = jnp.einsum("nd,nf->df", normed_two16, d_pre16, preferred_element_type=jnp.float32)
    d_expand_bias = jnp.sum(d_pre16.astype(jnp.float32), axis=0)
    d_normed_two = jnp.einsum("nf,df->nd", d_pre16, expand16, preferred_element_type=jnp.float32)
    d_resid_norm, d_gain_two, d_shift_two = norm_back_two(d_normed_two)
    d_residual = grad_out + d_resid_norm
    d_branch16 = d_residual.astype(jnp.bfloat16)
    d_proj = jnp.einsum("nd,ne->de", attended16, d_branch16, preferred_element_type=jnp.float32)
    d_proj_bias = jnp.sum(d_branch16.astype(jnp.float32), axis=0)
    d_attended16 = (
        jnp.einsum("ne,de->nd", d_branch16, proj16, preferred_element_type=jnp.float32)
        .astype(jnp.bfloat16)
        .reshape(images, tokens, D)
    )
    key_back, value_back = (key_all, value_all)

    def query_side(item_index):
        image_at = item_index // H
        head_at = item_index % H
        query_head = head_slice(query16, image_at, head_at)
        key_head = head_slice(key_back, image_at, head_at)
        value_head = head_slice(value_back, image_at, head_at)
        grad_head = head_slice(d_attended16, image_at, head_at)
        valid_keys = lax.dynamic_index_in_dim(key_valid, image_at, 0, keepdims=False)
        log_head = lax.dynamic_index_in_dim(log_totals, item_index, 0, keepdims=False)
        attn_full = jnp.exp(
            masked_scores(query_head, key_head, valid_keys, score_scale) - log_head[:, None]
        )
        d_probs = jnp.einsum("sd,ld->sl", grad_head, value_head, preferred_element_type=jnp.float32)
        inner_sum = jnp.sum(attn_full * d_probs, axis=-1, keepdims=True)
        d_scores = (attn_full * (d_probs - inner_sum)).astype(jnp.bfloat16)
        d_query = (
            jnp.einsum("sl,ld->sd", d_scores, key_head, preferred_element_type=jnp.float32)
            * score_scale
        )
        return (d_query, attn_full, d_scores, inner_sum[:, 0])

    def query_and_keys(item_index):
        image_at = item_index // H
        head_at = item_index % H
        query_head = head_slice(query16, image_at, head_at)
        grad_head = head_slice(d_attended16, image_at, head_at)
        d_query, attn_full, d_scores, inner_row = query_side(item_index)
        d_key = (
            jnp.einsum("sl,sd->ld", d_scores, query_head, preferred_element_type=jnp.float32)
            * score_scale
        )
        d_value = jnp.einsum(
            "sl,sd->ld",
            attn_full.astype(jnp.bfloat16),
            grad_head,
            preferred_element_type=jnp.float32,
        )
        return (d_query, d_key, d_value)

    d_query_items, d_key_items, d_value_items = lax.map(
        query_and_keys, jnp.arange(item_count, dtype=jnp.int32)
    )
    d_key_full = heads_last(d_key_items, images)
    d_value_full = heads_last(d_value_items, images)
    d_key_band, d_value_band = (
        lax.psum_scatter(d_key_full, "rows", scatter_dimension=1, tiled=True),
        lax.psum_scatter(d_value_full, "rows", scatter_dimension=1, tiled=True),
    )
    d_query_rot = heads_last(d_query_items, images).reshape(images, tokens, H, HD)
    d_queries, d_keys, d_freq = turn_back((d_query_rot, d_key_band.reshape(images, tokens, H, HD)))
    d_mixed16 = jnp.concatenate(
        [
            d_queries.reshape(rows_all, D),
            d_keys.reshape(rows_all, D),
            d_value_band.reshape(rows_all, D),
        ],
        axis=1,
    ).astype(jnp.bfloat16)
    d_qkv = jnp.einsum("nd,ne->de", normed16, d_mixed16, preferred_element_type=jnp.float32)
    d_qkv_bias = jnp.sum(d_mixed16.astype(jnp.float32), axis=0)
    d_normed = jnp.einsum("ne,de->nd", d_mixed16, qkv16, preferred_element_type=jnp.float32)
    d_flat, d_gain_one, d_shift_one = norm_back_one(d_normed)
    patch_grad = (d_residual + d_flat).reshape(images, band_rows, grid_w, D)
    gain_grad = jnp.stack([d_gain_one, d_gain_two])
    bias_grad = jnp.concatenate(
        [d_shift_one, d_shift_two, d_qkv_bias, d_proj_bias, d_expand_bias, d_shrink_bias]
    )
    shard_sizes = (
        qkv_weight.shape[1],
        proj_weight.shape[1],
        expand_weight.shape[1],
        shrink_weight.shape[0],
        gains_moment.shape[1],
        biases_moment.shape[0],
        freq_moment.shape[1],
    )
    shard_dims = (1, 1, 1, 0, 1, 0, 1)
    summed = lax.psum(
        (d_qkv, d_proj, d_expand, d_shrink, gain_grad, bias_grad, d_freq), ("batch", "rows")
    )
    reduced = tuple(
        (
            lax.dynamic_slice_in_dim(whole_grad, band_index * size_one, size_one, dim_one)
            for whole_grad, size_one, dim_one in zip(summed, shard_sizes, shard_dims)
        )
    )
    grad_qkv, grad_proj, grad_expand, grad_shrink, grad_gains, grad_biases, grad_freq = reduced
    qkv_moment_new = 0.5 * qkv_moment + grad_qkv
    proj_moment_new = 0.5 * proj_moment + grad_proj
    expand_moment_new = 0.5 * expand_moment + grad_expand
    shrink_moment_new = 0.5 * shrink_moment + grad_shrink
    gains_moment_new = 0.5 * gains_moment + grad_gains
    biases_moment_new = 0.5 * biases_moment + grad_biases
    freq_moment_new = 0.5 * freq_moment + grad_freq
    squares = jnp.stack(
        [
            jnp.sum(gains_moment_new * gains_moment_new),
            jnp.sum(biases_moment_new * biases_moment_new),
            jnp.sum(freq_moment_new * freq_moment_new),
        ]
    )
    current = [qkv_moment_new, proj_moment_new, expand_moment_new, shrink_moment_new.T]
    vector_totals = squares
    for sweep_index in range(5):
        partial_grams = [
            jnp.einsum("ik,jk->ij", column_block, column_block, precision=highest)
            for column_block in current
        ]
        extras = squares if sweep_index == 0 else jnp.zeros((3,), jnp.float32)
        gram_qkv, gram_proj, gram_expand, gram_shrink, extra_sum = lax.psum(
            (partial_grams[0], partial_grams[1], partial_grams[2], partial_grams[3], extras), "rows"
        )
        gram_list = [gram_qkv, gram_proj, gram_expand, gram_shrink]
        if sweep_index == 0:
            vector_totals = extra_sum
            frob_norms = [jnp.sqrt(jnp.trace(gram_one)) + 1e-07 for gram_one in gram_list]
            current = [
                column_block / frob_one for column_block, frob_one in zip(current, frob_norms)
            ]
            gram_list = [
                gram_one / (frob_one * frob_one)
                for gram_one, frob_one in zip(gram_list, frob_norms)
            ]
        current = [
            coeff_one * column_block
            + jnp.dot(
                coeff_two * gram_one + coeff_three * jnp.dot(gram_one, gram_one, precision=highest),
                column_block,
                precision=highest,
            )
            for column_block, gram_one in zip(current, gram_list)
        ]
    qkv_weight_new = qkv_weight - 0.05 * math.sqrt(3 * D) * current[0]
    proj_weight_new = proj_weight - 0.05 * math.sqrt(D) * current[1]
    expand_weight_new = expand_weight - 0.05 * math.sqrt(max(D, FF)) * current[2]
    shrink_weight_new = shrink_weight - 0.05 * math.sqrt(max(D, FF)) * current[3].T
    own_gains = lax.dynamic_slice_in_dim(
        norm_gains, band_index * gains_moment.shape[1], gains_moment.shape[1], 1
    )
    own_biases = lax.dynamic_slice_in_dim(
        all_biases, band_index * biases_moment.shape[0], biases_moment.shape[0], 0
    )
    own_freqs = lax.dynamic_slice_in_dim(
        frequencies, band_index * freq_moment.shape[1], freq_moment.shape[1], 1
    )
    norm_gains_new = own_gains - 0.2 * gains_moment_new * lax.rsqrt(
        vector_totals[0] / (2 * D) + 1e-06
    )
    all_biases_new = own_biases - 0.2 * biases_moment_new * lax.rsqrt(
        vector_totals[1] / (7 * D + FF) + 1e-06
    )
    frequencies_new = own_freqs - 0.2 * freq_moment_new * lax.rsqrt(
        vector_totals[2] / (H * HD) + 1e-06
    )
    return (
        block_out,
        patch_grad,
        qkv_moment_new,
        qkv_weight_new,
        proj_moment_new,
        proj_weight_new,
        expand_moment_new,
        expand_weight_new,
        shrink_moment_new,
        shrink_weight_new,
        gains_moment_new,
        norm_gains_new,
        biases_moment_new,
        all_biases_new,
        freq_moment_new,
        frequencies_new,
    )


def solution(mesh):
    placed = (
        P("batch", "rows", None, None),
        P("batch", "rows", None, None),
        P("batch"),
        P("batch"),
        P(None, "rows"),
        P(None, "rows"),
        P(None, "rows"),
        P(None, "rows"),
        P(None, "rows"),
        P(None, "rows"),
        P("rows", None),
        P("rows", None),
        P(),
        P(None, "rows"),
        P(),
        P("rows"),
        P(),
        P(None, "rows"),
    )
    return jax.shard_map(
        local,
        mesh=mesh,
        in_specs=placed,
        out_specs=(
            P("batch", "rows", None, None),
            P("batch", "rows", None, None),
            P(None, "rows"),
            P(None, "rows"),
            P(None, "rows"),
            P(None, "rows"),
            P(None, "rows"),
            P(None, "rows"),
            P("rows", None),
            P("rows", None),
            P(None, "rows"),
            P(None, "rows"),
            P("rows"),
            P("rows"),
            P(None, "rows"),
            P(None, "rows"),
        ),
        check_vma=False,
    )
```

profile of v0, /device:TPU:0, one launch (start us, length us, event | category | flops | bytes accessed | tf_op | source)
XLA Modules:
  0.0 1523.9 jit_solution(4689583626383171665)
XLA Ops:
  15.4 22.4 %all_gather.18 = bf16[384,1152]{0,1:T(8,128)(2,1)S(1)} all-gather(bf16[384,288]{0,1:T(8,128)(2,1)S(1)} %convert_element_type.137), channel_id=1, replica_groups=mesh['batch'=8,'rows'=4] {'rows'}, dimensions={1}, use_global_device_ids=true | all-gather | bytes 1105920 | tf_op jit(solution)/shard_map/all_gather | solution.py:102
  43.9 2.6 copy.92
  60.2 19.6 %all_gather.21 = bf16[384,384]{0,1:T(8,128)(2,1)} all-gather(bf16[384,96]{0,1:T(8,128)(2,1)S(1)} %convert_element_type.142), channel_id=1, replica_groups=mesh['batch'=8,'rows'=4] {'rows'}, dimensions={1}, use_global_device_ids=true | all-gather | bytes 368640 | tf_op jit(solution)/shard_map/all_gather | solution.py:103
  81.6 12.9 all-gather.5.cloned.1.call-done
  96.4 36.3 %all-gather.7.cloned.1.call-done = bf16[2,1024,384]{2,1,0:T(8,128)(2,1)} async-done(((bf16[2,256,384]{2,1,0:T(8,128)(2,1)}), bf16[2,1024,384]{2,1,0:T(8,128)(2,1)}) %all-gather.7.cloned.1.call-update) | async-done | bytes 1572880 | tf_op jit(solution)/shard_map/all_gather | solution.py:138
  132.7 73.9 %while.30 = (s32[]{:T(128)}, bf16[12,256,64]{1,2,0:T(8,128)(2,1)S(1)}, f32[12,256]{1,0:T(8,128)}, s32[12]{0:T(128)S(1)}, pred[2,1024]{1,0:T(4,128)(4,1)S(1)}, /*...) while((s32[]{:T(128)}, ...), condition=%wide.region_5.6_spmd, body=%wide.region_2.5_spmd.sunk | while | flops 69222160 | bytes 3784072 | solution.py:158
  209.6 10.8 multiply_convert_fusion.1
  220.4 5.7 convert_reduce_fusion
  230.8 133.0 %while.31 = (s32[]{:T(128)}, f32[12,256,64]{1,2,0:T(8,128)}, f32[12,1024,64]{1,2,0:T(8,128)}, f32[12,1024,64]{1,2,0:T(8,128)}, s32[12]{0:T(128)}, /*index=5*/pre...) while((s32[]{:T(128)}, f32[12,256,64]{1,2,0:T(8,128)}, ...), condition=%wide.region_12.13_spmd, body=%wide.region_10.12_spmd.sunk | while | flops 170213136 | bytes 9515474 | solution.py:236
  364.4 6.0 copy.104
  370.4 95.3 %copy.116 = f32[2,1024,384]{0,2,1:T(8,128)} copy(f32[2,1024,384]{1,0,2:T(2,128)} %bitcast.332) | data formatting | bytes 6291456
  465.6 142.4 %reshape.500 = f32[1024,768]{1,0:T(8,128)} reshape(f32[1024,384,2]{2,1,0:T(8,128)} %bitcast.48) | data formatting | bytes 6291456
  608.1 2.8 copy.135
  618.1 6.0 multiply_reduce_fusion.12
  624.9 42.5 %reduce-scatter.7.cloned.1.call-done = f32[256,768]{1,0:T(8,128)} async-done(((f32[1024,768]{1,0:T(8,128)}), f32[256,768]{1,0:T(8,128)}) %reduce-scatter.7.cloned.1.call-update) | async-done | bytes 786448
  667.4 56.4 %reshape.501 = bf16[256,384,2]{2,1,0:T(8,128)(2,1)} reshape(f32[256,768]{1,0:T(8,128)} %reduce-scatter.7.cloned.1.call-done) | data formatting | bytes 1179648
  723.7 23.3 %copy.117 = bf16[2,256,384]{1,0,2:T(2,128)(2,1)S(1)} copy(bf16[2,256,384]{0,2,1:T(8,128)(2,1)} %bitcast.330) | data formatting | bytes 786432
  753.0 161.4 %all-reduce.20.cloned.1.call-done = (f32[384,1152]{0,1:T(8,128)}, f32[384,384]{0,1:T(8,128)}, f32[384,1536]{1,0:T(8,128)}, f32[1536,384]{0,1:T(8,128)}) async-done(((f32[384,1152]{0,1:T(8,128)}, f32[384,384]{0,1:T(8,128)}, f32[384,1536]{1,0:T(8,128)}, f32[1536,384]{0,1:T(8,128)}), (f32[384,1152]{0,1:T(8,128)}, f32[384,384]{0,1:T(8,128)}, f32[384,1536]{1,0:T(8,128)}, ...) | async-done | bytes 7077904 | tf_op jit(solution)/shard_map/psum | solution.py:274
  926.8 96.9 %all-reduce.30.cloned.1.call-done = (f32[384,384]{1,0:T(8,128)}, f32[384,384]{1,0:T(8,128)}, f32[384,384]{1,0:T(8,128)}, f32[384,384]{1,0:T(8,128)}) async-done(((f32[384,384]{1,0:T(8,128)}, f32[384,384]{1,0:T(8,128)}, f32[384,384]{1,0:T(8,128)}, f32[384,384]{1,0:T(8,128)}), (f32[384,384]{1,0:T(8,128)}, f32[384,384]{1,0:T(8,128)}, f32[384,384]{1,0:T(8,128)}, ...) | async-done | bytes 2359312 | tf_op jit(solution)/shard_map/psum | solution.py:306
  1033.3 2.9 fusion.50
  1053.6 95.8 %all-reduce.28.cloned.1.call-done = (f32[384,384]{1,0:T(8,128)}, f32[384,384]{1,0:T(8,128)}, f32[384,384]{1,0:T(8,128)}, f32[384,384]{1,0:T(8,128)}) async-done(((f32[384,384]{1,0:T(8,128)}, f32[384,384]{1,0:T(8,128)}, f32[384,384]{1,0:T(8,128)}, f32[384,384]{1,0:T(8,128)}), (f32[384,384]{1,0:T(8,128)}, f32[384,384]{1,0:T(8,128)}, f32[384,384]{1,0:T(8,128)}, ...) | async-done | bytes 2359312 | tf_op jit(solution)/shard_map/psum | solution.py:306
  1149.4 2.9 fusion.51
  1169.9 95.8 %all-reduce.26.cloned.1.call-done = (f32[384,384]{1,0:T(8,128)}, f32[384,384]{1,0:T(8,128)}, f32[384,384]{1,0:T(8,128)}, f32[384,384]{1,0:T(8,128)}) async-done(((f32[384,384]{1,0:T(8,128)}, f32[384,384]{1,0:T(8,128)}, f32[384,384]{1,0:T(8,128)}, f32[384,384]{1,0:T(8,128)}), (f32[384,384]{1,0:T(8,128)}, f32[384,384]{1,0:T(8,128)}, f32[384,384]{1,0:T(8,128)}, ...) | async-done | bytes 2359312 | tf_op jit(solution)/shard_map/psum | solution.py:306
  1265.6 2.7 fusion.52
  1299.4 42.6 %all-reduce.6 = (f32[2,384]{1,0:T(2,128)S(1)}, f32[2,192]{1,0:T(2,128)S(1)}, f32[4224]{0:T(1024)S(1)}) all-reduce(f32[2,384]{1,0:T(2,128)S(1)} %pad_maximum_fusion.2, f32[2,192]{1,0:T(2,128)S(1)} %pad_add_fusion, f32[4224]{0:T(1024)S(1)} %constant_dynamic-update-slice_fusion.6), channel_id=1, replica_groups=mesh['batch'=8,'rows'=4] {'batch','rows'}, use_global_device_ids=true, to_apply=%region_47.48 | all-reduce | flops 5376 | bytes 43008 | tf_op jit(solution)/shard_map/psum | solution.py:274
  1342.1 41.3 %all-reduce.24.cloned.1.call-done = (f32[384,384]{1,0:T(8,128)}, f32[384,384]{1,0:T(8,128)}, f32[384,384]{1,0:T(8,128)}, f32[384,384]{1,0:T(8,128)}) async-done(((f32[384,384]{1,0:T(8,128)}, f32[384,384]{1,0:T(8,128)}, f32[384,384]{1,0:T(8,128)}, f32[384,384]{1,0:T(8,128)}), (f32[384,384]{1,0:T(8,128)}, f32[384,384]{1,0:T(8,128)}, f32[384,384]{1,0:T(8,128)}, ...) | async-done | bytes 2359312 | tf_op jit(solution)/shard_map/psum | solution.py:306
  1383.4 2.8 fusion.53
  1411.6 3.6 fusion.74
  1415.2 10.3 psum.223
  1437.8 64.0 %all-reduce.22.cloned.1.call-done = (f32[384,384]{1,0:T(8,128)}, f32[384,384]{1,0:T(8,128)}, f32[384,384]{1,0:T(8,128)}, f32[384,384]{1,0:T(8,128)}) async-done(((f32[384,384]{1,0:T(8,128)}, f32[384,384]{1,0:T(8,128)}, f32[384,384]{1,0:T(8,128)}, f32[384,384]{1,0:T(8,128)}), (f32[384,384]{1,0:T(8,128)}, f32[384,384]{1,0:T(8,128)}, f32[384,384]{1,0:T(8,128)}, ...) | async-done | bytes 2359312 | tf_op jit(solution)/shard_map/psum | solution.py:306
  1501.8 2.9 fusion.54
  1514.0 2.9 fusion.73
  (636 shorter events, 318.2 us)
Async XLA Ops:
  7.2 87.3 %all-gather.5.cloned.1.call-start = ((), (), s32[]{:S(2)}) async-start(), calls=%async_computation.2 | async-start | bytes 1966080 | tf_op jit(solution)/shard_map/all_gather | solution.py:137
  8.5 31.6 %copy-start.88 = (f32[512]{0:T(512)}, f32[512]{0:T(512)S(1)}, u32[]{:S(2)}) copy-start(f32[512]{0:T(512)S(1)} %div.129) | copy-start | bytes 6148
  12.7 36.3 %copy-start.81 = (f32[6,32]{1,0:T(8,128)}, f32[6,32]{1,0:T(8,128)S(1)}, u32[]{:S(2)}) copy-start(f32[6,32]{1,0:T(8,128)S(1)} %mul.781) | copy-start | bytes 2308
  13.3 35.7 %copy-start.105 = (f32[256]{0:T(256)}, f32[256]{0:T(256)S(1)}, u32[]{:S(2)}) copy-start(f32[256]{0:T(256)S(1)} %convert_element_type.138) | copy-start | bytes 3076
  13.3 35.6 %copy-start.83 = (f32[6,32]{1,0:T(8,128)}, f32[6,32]{1,0:T(8,128)S(1)}, u32[]{:S(2)}) copy-start(f32[6,32]{1,0:T(8,128)S(1)} %mul.785) | copy-start | bytes 2308
  13.4 35.6 %copy-start.106 = (f32[256]{0:T(256)}, f32[256]{0:T(256)S(1)}, u32[]{:S(2)}) copy-start(f32[256]{0:T(256)S(1)} %convert_element_type.139) | copy-start | bytes 3076
  53.4 79.3 %all-gather.7.cloned.1.call-start = ((), (), s32[]{:S(2)}) async-start(), calls=%async_computation.3 | async-start | bytes 1966080 | tf_op jit(solution)/shard_map/all_gather | solution.py:138
  54.2 155.4 %all-gather.9.cloned.1.call-start = ((), (), s32[]{:S(2)}) async-start(), calls=%async_computation.4 | async-start | bytes 1474560 | tf_op jit(solution)/shard_map/all_gather | solution.py:104
  56.1 164.2 %all-gather.11.cloned.1.call-start = ((), (), s32[]{:S(2)}) async-start(), calls=%async_computation.5 | async-start | bytes 1474560 | tf_op jit(solution)/shard_map/all_gather | solution.py:105
  58.0 558.9 %reduce-scatter.5.cloned.1.call-start = ((), (), s32[]{:S(2)}) async-start(), calls=%async_computation.6 | async-start | bytes 3932160 | tf_op jit(solution)/shard_map/reduce_scatter | solution.py:242
  60.1 36.3 %copy-start.103 = (bf16[1,2,2,128]{3,1,2,0:T(2,128)(2,1)}, bf16[1,2,2,128]{3,1,2,0:T(2,128)(2,1)S(1)}, u32[]{:S(2)}) copy-start(bf16[1,2,2,128]{3,1,2,0:T(2,128)(2,1)S(1)} %copy.122) | copy-start | bytes 3076
  132.7 74.3 %copy-start = (bf16[2,8,32,384]{3,2,1,0:T(8,128)(2,1)S(1)}, bf16[2,8,32,384]{3,2,1,0:T(8,128)(2,1)}, u32[]{:S(2)}) copy-start(bf16[2,8,32,384]{3,2,1,0:T(8,128)(2,1)} %param.22) | copy-start | bytes 1179652
  132.7 74.4 %copy-start.109 = (f32[384]{0:T(512)S(1)}, f32[384]{0:T(512)}, u32[]{:S(2)}) copy-start(f32[384]{0:T(512)} %get-tuple-element.515) | copy-start | bytes 4612
  363.9 303.5 %reduce-scatter.7.cloned.1.call-start = ((), (), s32[]{:S(2)}) async-start(), calls=%async_computation.7 | async-start | bytes 3932160
  608.1 306.4 %all-reduce.20.cloned.1.call-start = ((), (), s32[]{:S(2)}) async-start(), calls=%async_computation.8 | async-start | bytes 14155776 | tf_op jit(solution)/shard_map/psum | solution.py:274
  749.3 165.2 %copy-start.80 = (f32[384,96]{0,1:T(8,128)S(1)}, f32[384,96]{0,1:T(8,128)}, u32[]{:S(2)}) copy-start(f32[384,96]{0,1:T(8,128)} %param.29) | copy-start | bytes 442372
  749.3 274.3 %all-reduce.30.cloned.1.call-start = ((), (), s32[]{:S(2)}) async-start(), calls=%async_computation.13 | async-start | bytes 4718592 | tf_op jit(solution)/shard_map/psum | solution.py:306
  751.7 168.6 %copy-start.61 = (f32[384,384]{1,0:T(8,128)S(1)}, f32[384,384]{1,0:T(8,128)}, u32[]{:S(2)}) copy-start(f32[384,384]{1,0:T(8,128)} %copy.106) | copy-start | bytes 1769476
  915.4 123.2 %copy-start.71 = (f32[384,96]{0,1:T(8,128)}, f32[384,96]{0,1:T(8,128)S(1)}, u32[]{:S(2)}) copy-start(f32[384,96]{0,1:T(8,128)S(1)} %dynamic-slice_add_fusion.3) | copy-start | bytes 442372
  918.1 118.1 %copy-start.28 = (f32[384,288]{0,1:T(8,128)}, f32[384,288]{0,1:T(8,128)S(1)}, u32[]{:S(2)}) copy-start(f32[384,288]{0,1:T(8,128)S(1)} %dynamic-slice_add_fusion.2) | copy-start | bytes 1327108
  921.4 119.2 %copy-start.26 = (f32[384,384]{1,0:T(8,128)}, f32[384,384]{1,0:T(8,128)S(1)}, u32[]{:S(2)}) copy-start(f32[384,384]{1,0:T(8,128)S(1)} %dynamic-slice_add_fusion.1) | copy-start | bytes 1769476
  926.7 222.7 %all-reduce.28.cloned.1.call-start = ((), (), s32[]{:S(2)}) async-start(), calls=%async_computation.12 | async-start | bytes 4718592 | tf_op jit(solution)/shard_map/psum | solution.py:306
  1053.6 212.1 %all-reduce.26.cloned.1.call-start = ((), (), s32[]{:S(2)}) async-start(), calls=%async_computation.11 | async-start | bytes 4718592 | tf_op jit(solution)/shard_map/psum | solution.py:306
  1169.8 98.6 %copy-start.14 = (f32[384,288]{0,1:T(8,128)S(1)}, f32[384,288]{0,1:T(8,128)}, u32[]{:S(2)}) copy-start(f32[384,288]{0,1:T(8,128)} %copy-done.13) | copy-start | bytes 1327108
  1169.8 213.6 %all-reduce.24.cloned.1.call-start = ((), (), s32[]{:S(2)}) async-start(), calls=%async_computation.10 | async-start | bytes 4718592 | tf_op jit(solution)/shard_map/psum | solution.py:306
  1286.6 215.2 %all-reduce.22.cloned.1.call-start = ((), (), s32[]{:S(2)}) async-start(), calls=%async_computation.9 | async-start | bytes 4718592 | tf_op jit(solution)/shard_map/psum | solution.py:306
  1297.1 89.1 %copy-start.12 = (f32[384,288]{0,1:T(8,128)S(1)}, f32[384,288]{0,1:T(8,128)}, u32[]{:S(2)}) copy-start(f32[384,288]{0,1:T(8,128)} %copy-done.11) | copy-start | bytes 1327108
  1297.2 93.0 %copy-start.101 = (f32[512]{0:T(512)}, f32[512]{0:T(512)S(1)}, u32[]{:S(2)}) copy-start(f32[512]{0:T(512)S(1)} %multiply_multiply_fusion.5) | copy-start | bytes 6148
  1432.9 71.9 %copy-start.18 = (f32[384,288]{0,1:T(8,128)S(1)}, f32[384,288]{0,1:T(8,128)}, u32[]{:S(2)}) copy-start(f32[384,288]{0,1:T(8,128)} %copy-done.17) | copy-start | bytes 1327108
  1435.4 69.3 %copy-start.66 = (f32[384,288]{0,1:T(8,128)S(1)}, f32[384,288]{0,1:T(8,128)}, u32[]{:S(2)}) copy-start(f32[384,288]{0,1:T(8,128)} %param.26) | copy-start | bytes 1327108
  1436.5 71.4 %copy-start.47 = (f32[384,96]{0,1:T(8,128)S(1)}, f32[384,96]{0,1:T(8,128)}, u32[]{:S(2)}) copy-start(f32[384,96]{0,1:T(8,128)} %copy-done.46) | copy-start | bytes 442372
  1436.5 71.4 %copy-start.79 = (f32[384,96]{0,1:T(8,128)S(1)}, f32[384,96]{0,1:T(8,128)}, u32[]{:S(2)}) copy-start(f32[384,96]{0,1:T(8,128)} %param.28) | copy-start | bytes 442372
  (99 other events, 622.6 us)
Sparse Core Ops, SparseCore 0:
  53.5 40.9 all-gather.4
  96.6 36.0 all-gather.6
  134.9 29.0 all-gather.8
  166.0 29.7 all-gather.10
  364.0 59.0 reduce-scatter.4
  608.2 59.1 reduce-scatter.6
  749.4 164.9 all-reduce.19
  926.9 96.7 all-reduce.29
  1053.7 95.6 all-reduce.27
  1169.9 95.6 all-reduce.25
  1286.8 96.6 all-reduce.23
  1406.0 95.8 all-reduce.21
where the time goes:
time: 1540 us; the launch traced here: 1520 us
  waiting for transfers between devices  647 us (42%)
  local copies, waits for them, and re-layouts  408 us (26%)
  matrix products  221 us (14%)
  blocking collectives  94.9 us (6%)
  loops' own time  71.1 us (5%)
  other arithmetic  58.9 us (4%)
  between operations  20.9 us (1%)
    psum x5, waiting for transfers between devices, local(): lax.psum((partial_grams[0], partial_grams[1], partial_grams[2], partial_g...  394 us
    unnamed x258, local copies, waits for them, and re-layouts  328 us
    psum x1, waiting for transfers between devices, local(): lax.psum((d_qkv, d_proj, d_expand, d_shrink, gain_grad, bias_grad, d_freq...  161 us
    another operation x1, loops' own time, local(): lax.map(query_and_keys, jnp.arange(item_count, dtype=jnp.int32))  47.2 us
    unnamed x13, waiting for transfers between devices  42.7 us
    psum x1, blocking collectives, local(): lax.psum((d_qkv, d_proj, d_expand, d_shrink, gain_grad, bias_grad, d_freq...  42.6 us
    dot_general x20, matrix products, local(): jnp.einsum('ik,jk->ij', column_block, column_block, precision=highest)  39.2 us
    all_gather x1, waiting for transfers between devices, local(): lax.all_gather(values16, 'rows', axis=1, tiled=True)  36.3 us
  transfers between devices with their start and end apart: 12, of which 9 were waited for; matrix products, arithmetic and copies ran while one was open for 24% of the time, Pallas kernels for 0%

commit v1 on v0

v1 whole, which is shorter than its diff:
```python
import functools
import math

import jax
import jax.numpy as jnp
from jax import lax
from jax.experimental import pallas as pl
from jax.experimental.pallas import tpu as pltpu
from jax.sharding import PartitionSpec as P

D = 384
H = 6
HD = 64
FF = 1536
HALF = HD // 2
OWN_HEADS = H // 2
OWN = OWN_HEADS * HD
AUG = HD + 16

coeff_one = 3.4445
coeff_two = -4.775
coeff_three = 2.0315

bf16 = jnp.bfloat16
f32 = jnp.float32
AXES = ("batch", "rows")


def dot_nn(a, b):
    return lax.dot_general(a, b, (((1,), (0,)), ((), ())), preferred_element_type=f32)


def dot_nt(a, b):
    return lax.dot_general(a, b, (((1,), (1,)), ((), ())), preferred_element_type=f32)


def dot_tn(a, b):
    return lax.dot_general(a, b, (((0,), (0,)), ((), ())), preferred_element_type=f32)


def kernel_call(body, out_shape, scratch=(), smem=0, n_in=0, limit=52):
    specs = [pl.BlockSpec(memory_space=pltpu.SMEM)] * smem
    specs += [pl.BlockSpec(memory_space=pltpu.VMEM)] * n_in
    return pl.pallas_call(
        body,
        out_shape=out_shape,
        in_specs=specs,
        out_specs=jax.tree.map(lambda _: pl.BlockSpec(memory_space=pltpu.VMEM), out_shape),
        scratch_shapes=list(scratch),
        compiler_params=pltpu.CompilerParams(vmem_limit_bytes=limit * 2**20),
    )


def sds(shape, dtype):
    return jax.ShapeDtypeStruct(shape, dtype)


def norm_rows(x):
    centered = x - jnp.mean(x, axis=-1, keepdims=True)
    rstd = lax.rsqrt(jnp.mean(centered * centered, axis=-1, keepdims=True) + 1e-06)
    return centered * rstd, rstd


def half_blocks(core, shard):
    if isinstance(shard, int):
        base = jnp.where(core == 0, (0, 4, 8, 10)[shard], (0, 2, 4, 8)[shard])
        count = jnp.where(core == 0, (4, 4, 2, 2)[shard], (2, 2, 4, 4)[shard])
        return base, count
    raise TypeError(shard)


def front_kernel(
    pos, own_a, own_b, oth_a, oth_b, w0, w1, w2, w3, bias, gain, shift, cos, sin, rows, cols,
    normed, w_own, qrot, krot, q_aug, k_aug, k_nat, v_nat, logs, o_own, o_oth,
    w_all, v_t, o_all,
):
    core, band, chip = pos[0], pos[1], pos[2]
    tokens = normed.shape[0]
    half = tokens // 2
    block = 256
    for e, ref in enumerate((w0, w1, w2, w3)):
        quarter = lax.bitwise_xor(chip, e)
        for shard in range(4):
            base, count = half_blocks(core, shard)
            at = jnp.where(quarter < count, base + quarter, 12)
            w_all[pl.ds(pl.multiple_of(at * 48, 16), 48), :] = ref[lax.bitwise_xor(band, shard)]
    w_own[...] = w_all[0 : 3 * OWN, :]
    for b, src in enumerate((own_a, own_b, oth_a, oth_b)):
        xhat, _ = norm_rows(src[0:block, :].astype(f32))
        normed[b * block : (b + 1) * block, :] = (xhat * gain[...] + shift[...]).astype(bf16)
    high = own_a[block : block + 1, 0:1].astype(f32)
    wide = own_a[block + 1 : block + 2, 0:1].astype(f32)
    inside = jnp.logical_and(rows[...] < high, cols[...] < wide)
    key_bias = jnp.where(inside, 0.0, -1e9).astype(f32)
    ones_row = (lax.broadcasted_iota(jnp.int32, (AUG - HD, block), 0) == 0).astype(f32)
    for b in range(tokens // block):
        here = slice(b * block, (b + 1) * block)
        mixed = dot_nt(w_own[...], normed[here, :]) + bias[...]
        for h in range(OWN_HEADS):
            c = cos[h * HALF : (h + 1) * HALF, here]
            s = sin[h * HALF : (h + 1) * HALF, here]
            qu = mixed[h * HD : h * HD + HALF, :]
            qw = mixed[h * HD + HALF : (h + 1) * HD, :]
            ku = mixed[OWN + h * HD : OWN + h * HD + HALF, :]
            kw = mixed[OWN + h * HD + HALF : OWN + (h + 1) * HD, :]
            qr = jnp.concatenate([qu * c - qw * s, qw * c + qu * s], axis=0)
            kr = jnp.concatenate([ku * c - kw * s, kw * c + ku * s], axis=0)
            qrot[h * HD : (h + 1) * HD, here] = qr
            krot[h * HD : (h + 1) * HD, here] = kr
            q_low = qr.astype(bf16).astype(f32) * 0.125
            q_aug[h, :, here] = jnp.concatenate([q_low, ones_row], axis=0).astype(bf16)
            k_full = jnp.concatenate([kr, ones_row * key_bias[:, here]], axis=0)
            k_aug[h, :, here] = k_full.astype(bf16)
            k_nat[h, here, :] = k_full.T.astype(bf16)
            vv = mixed[2 * OWN + h * HD : 2 * OWN + (h + 1) * HD, :]
            v_t[h, :, here] = vv.astype(bf16)
            v_nat[h, here, :] = vv.T.astype(bf16)

    blocks = tokens // block

    def attend(item, carry):
        h = item // blocks
        at = pl.multiple_of(lax.rem(item, blocks) * block, block)
        here = pl.ds(at, block)
        scores = dot_nn(k_nat[h], q_aug[h, :, here])
        peak = jnp.max(scores, axis=0, keepdims=True)
        e = jnp.exp(scores - peak)
        total = jnp.sum(e, axis=0, keepdims=True)
        out = dot_nn(v_t[h], (e * (1.0 / total)).astype(bf16))
        logs[h, :, here] = peak + jnp.log(total)
        o_all[h, :, here] = out.astype(bf16)
        return carry

    lax.fori_loop(0, OWN_HEADS * blocks, attend, 0)
    for h in range(OWN_HEADS):
        o_own[h * HD : (h + 1) * HD, :] = o_all[h, :, 0:half]
        o_oth[h * HD : (h + 1) * HD, :] = o_all[h, :, half:tokens]


def front(pos, slabs, weights, bias, gain, shift, cos, sin, rows, cols):
    tokens = rows.shape[1]
    half = tokens // 2
    nh = OWN_HEADS
    outs = (
        sds((tokens, D), bf16),
        sds((3 * OWN, D), bf16),
        sds((OWN, tokens), f32),
        sds((OWN, tokens), f32),
        sds((nh, AUG, tokens), bf16),
        sds((nh, AUG, tokens), bf16),
        sds((nh, tokens, AUG), bf16),
        sds((nh, tokens, HD), bf16),
        sds((nh, 1, tokens), f32),
        sds((OWN, half), bf16),
        sds((OWN, half), bf16),
    )
    scratch = [
        pltpu.VMEM((3 * OWN + 48, D), bf16),
        pltpu.VMEM((nh, HD, tokens), bf16),
        pltpu.VMEM((nh, HD, tokens), bf16),
    ]
    return kernel_call(front_kernel, outs, scratch, 1, 15)(
        pos, *slabs, *weights, bias, gain, shift, cos, sin, rows, cols
    )


def middle_kernel(
    pos, own_a, own_b, cot_a, cot_b, row_col, att_mine, att_oth,
    m0, m1, m2, m3, t0, t1, t2, t3, gain, shift, proj_bias, expand_bias, shrink_bias,
    block_out, d_residual, d_mine, d_send, keep, send, vec,
    p_all, e_one, s_one, att, resid, xhat_s, rstd_s, n2, g16, pre, dh, hidden, dpre, acc, dn2, dat, valid,
):
    core, band, chip = pos[0], pos[1], pos[2]
    half = block_out.shape[0]
    slab = half // 2
    att_t = jnp.concatenate(
        [
            jnp.where(core == 0, att_mine[...].astype(f32), att_oth[...].astype(f32)),
            jnp.where(core == 0, att_oth[...].astype(f32), att_mine[...].astype(f32)),
        ],
        axis=0,
    )
    att[...] = att_t.T.astype(bf16)
    pieces = []
    for e, (mine, other) in enumerate(((m0, t0), (m1, t1), (m2, t2), (m3, t3))):
        chip_e = lax.bitwise_xor(chip, e)
        pieces.append((mine, chip_e * 2 + core))
        pieces.append((other, chip_e * 2 + 1 - core))
    for ref, piece in pieces:
        for d in range(4):
            shard = lax.bitwise_xor(band, d)
            at = jnp.where(piece < 6, shard * 6 + piece, 24)
            p_all[pl.ds(pl.multiple_of(at * 16, 16), 16), :] = ref[d, 0:16, :]
    high = own_a[slab : slab + 1, 0:1].astype(f32)
    wide = own_a[slab + 1 : slab + 2, 0:1].astype(f32)
    inside = jnp.logical_and(row_col[:, 0:1] < high, row_col[:, 1:2] < wide)
    valid[...] = inside.astype(f32)
    g16[0:slab, :] = (cot_a[...].astype(f32) * valid[0:slab, :]).astype(bf16)
    g16[slab:half, :] = (cot_b[...].astype(f32) * valid[slab:half, :]).astype(bf16)
    rows = 128
    proj = p_all[0:D, :]
    for b in range(half // rows):
        here = slice(b * rows, (b + 1) * rows)
        src = own_a if b * rows < slab else own_b
        at = (b * rows) % slab
        res = src[at : at + rows, :].astype(f32) + dot_nt(att[here, :], proj) + proj_bias[...]
        resid[here, :] = res
        xhat, rstd = norm_rows(res)
        xhat_s[here, :] = xhat
        rstd_s[here, :] = rstd
        n2[here, :] = (xhat * gain[...] + shift[...]).astype(bf16)
    acc[...] = jnp.zeros_like(acc)
    dn2[...] = jnp.zeros_like(dn2)
    vec[...] = jnp.zeros_like(vec)

    def chunk(j, carry):
        d = lax.bitwise_xor(band, j)
        for ref, piece in pieces:
            at = pl.ds(pl.multiple_of(piece * 48, 16), 48)
            e_one[at, :] = ref[d, 16:64, :]
            s_one[at, :] = ref[d, 64:112, :]
        pre[...] = dot_nt(n2[...], e_one[...]) + expand_bias[j]
        dh[...] = dot_nt(g16[...], s_one[...])
        for b in range(half // 64):
            here = slice(b * 64, (b + 1) * 64)
            x = pre[here, :]
            cdf = 0.5 * (1.0 + lax.erf(x * math.sqrt(0.5)))
            hidden[here, :] = (x * cdf).astype(bf16)
            slope = cdf + x * (jnp.exp(-0.5 * x * x) * (1.0 / math.sqrt(2.0 * math.pi)))
            dpre[here, :] = (dh[here, :] * slope).astype(bf16)
        acc[...] += dot_nn(hidden[...], s_one[...])
        dn2[...] += dot_nn(dpre[...], e_one[...])
        vec[pl.ds(8 + j, 1), :] = jnp.sum(dpre[...].astype(f32), axis=0, keepdims=True)
        grad_s = dot_tn(hidden[...], g16[...])
        grad_e = dot_tn(dpre[...], n2[...])
        first = core == 0
        kept = jnp.where(first, grad_s, grad_e)
        sent = jnp.where(first, grad_e, grad_s).astype(bf16)
        for q in range(4):
            keep[q, j, 0:96, :] = kept[q * 96 : (q + 1) * 96, :]
            send[q, j, 0:96, :] = sent[q * 96 : (q + 1) * 96, :]
        return carry

    lax.fori_loop(0, 4, chunk, 0)
    block_out[...] = ((resid[...] + acc[...] + shrink_bias[...]) * valid[...]).astype(bf16)
    g = g16[...].astype(f32)
    vec[12:13, :] = jnp.sum(g, axis=0, keepdims=True)
    dn = dn2[...]
    xhat = xhat_s[...]
    vec[3:4, :] = jnp.sum(dn, axis=0, keepdims=True)
    vec[1:2, :] = jnp.sum(dn * xhat, axis=0, keepdims=True)
    dx = dn * gain[...]
    back_x = rstd_s[...] * (
        dx - jnp.mean(dx, axis=-1, keepdims=True) - xhat * jnp.mean(dx * xhat, axis=-1, keepdims=True)
    )
    d_res = g + back_x
    d_residual[...] = d_res
    branch = d_res.astype(bf16)
    vec[7:8, :] = jnp.sum(branch.astype(f32), axis=0, keepdims=True)
    grad_p = dot_tn(branch, att[...])
    rest = jnp.zeros((8, D), f32)
    for z in range(4):
        for q in range(4):
            at = z * 96 + q * 24
            padded = jnp.concatenate([grad_p[at : at + 24, :], rest], axis=0).astype(bf16)
            send[q, z, 96:128, :] = padded
            keep[q, z, 96:128, :] = padded.astype(f32)
    d_att = dot_nn(branch, proj)
    dat[...] = d_att.T.astype(bf16)
    d_mine[...] = dat[pl.ds(pl.multiple_of(core * OWN, 16), OWN), :]
    d_send[...] = dat[pl.ds(pl.multiple_of((1 - core) * OWN, 16), OWN), :]


def middle(pos, own, cot, row_col, att, mine, other, gain, shift, pb, eb, sb):
    half = row_col.shape[0]
    outs = (
        sds((half, D), bf16),
        sds((half, D), f32),
        sds((OWN, half), bf16),
        sds((OWN, half), bf16),
        sds((4, 4, 128, D), f32),
        sds((4, 4, 128, D), bf16),
        sds((16, D), f32),
    )
    v = pltpu.VMEM
    scratch = [
        v((D + 16, D), bf16), v((D, D), bf16), v((D, D), bf16), v((half, D), bf16), v((half, D), f32),
        v((half, D), f32), v((half, 1), f32), v((half, D), bf16), v((half, D), bf16), v((half, D), f32),
        v((half, D), f32), v((half, D), bf16), v((half, D), bf16), v((half, D), f32), v((half, D), f32),
        v((D, half), bf16), v((half, 1), f32),
    ]
    return kernel_call(middle_kernel, outs, scratch, 1, 20)(
        pos, *own, *cot, row_col, *att, *mine, *other, gain, shift, pb, eb, sb
    )


def merge_kernel(pos, keep, recv, mine, s1, s2, s3):
    chip = pos[2]

    def add(z, carry):
        mine[z] = keep[chip, z] + recv[chip, z].astype(f32)
        for e, ref in ((1, s1), (2, s2), (3, s3)):
            at = lax.bitwise_xor(chip, e)
            ref[z] = (keep[at, z] + recv[at, z].astype(f32)).astype(bf16)
        return carry

    lax.fori_loop(0, 4, add, 0)


def merge(pos, keep, recv):
    shape = keep.shape[1:]
    outs = (sds(shape, f32),) + (sds(shape, bf16),) * 3
    return kernel_call(merge_kernel, outs, (), 1, 2)(pos, keep, recv)


def bands_kernel(pos, mine, r1, r2, r3, own, s1, s2, s3):
    band = pos[1]
    for d, ref in ((0, own), (1, s1), (2, s2), (3, s3)):
        z = lax.bitwise_xor(band, d)
        part = (mine[z] + r1[z].astype(f32)) + (r2[z].astype(f32) + r3[z].astype(f32))
        ref[...] = part.astype(ref.dtype)


def bands(pos, mine, received):
    shape = mine.shape[1:]
    outs = (sds(shape, f32),) + (sds(shape, bf16),) * 3
    return kernel_call(bands_kernel, outs, (), 1, 4)(pos, mine, *received)


def piece_kernel(own, r1, r2, r3, mom, out):
    total = (own[...] + r1[...].astype(f32)) + (r2[...].astype(f32) + r3[...].astype(f32))
    out[...] = (total + 0.5 * mom[...]).astype(bf16)


def piece_sum(own, received, mom):
    return kernel_call(piece_kernel, sds(own.shape, bf16), (), 0, 5)(own, *received, mom)


def sum_low_kernel(own, r1, r2, r3, out):
    out[...] = ((own[...].astype(f32) + r1[...].astype(f32)) + (r2[...].astype(f32) + r3[...].astype(f32))).astype(bf16)


def sum_low(own, received):
    return kernel_call(sum_low_kernel, sds(own.shape, bf16), (), 0, 4)(own, *received)


def back_step(k_nat, v_nat, k_t, q_t, g, logs):
    p = jnp.exp(dot_nn(k_nat, q_t) - logs)
    dp = dot_nn(v_nat, g)
    inner = jnp.sum(p * dp, axis=0, keepdims=True)
    ds = (p * (dp - inner)).astype(bf16)
    dv = dot_nt(p.astype(bf16), g)
    dk = dot_nt(ds, q_t[0:HD, :])
    dq = dot_nn(k_t, ds) * 0.125
    return dq, dk, dv


def back_heads_kernel(heads, q_aug, k_aug, k_nat, v_nat, logs, d_mine, d_recv, dq, dk, dv, d_out):
    tokens = q_aug.shape[2]
    half = tokens // 2
    block = 256
    blocks = tokens // block
    count = heads[1] - heads[0]
    for i in range(count):
        h = heads[0] + i
        d_out[i, :, 0:half] = d_mine[h * HD : (h + 1) * HD, :]
        d_out[i, :, half:tokens] = d_recv[h * HD : (h + 1) * HD, :]
    dk[...] = jnp.zeros_like(dk)
    dv[...] = jnp.zeros_like(dv)

    def step(item, carry):
        i = item // blocks
        h = heads[0] + i
        at = pl.multiple_of(lax.rem(item, blocks) * block, block)
        here = pl.ds(at, block)
        dq_one, dk_one, dv_one = back_step(
            k_nat[h], v_nat[h], k_aug[h, 0:HD, :], q_aug[h, :, here], d_out[i, :, here], logs[h, :, here]
        )
        dv[i] += dv_one
        dk[i] += dk_one
        dq[i, :, here] = dq_one
        return carry

    lax.fori_loop(0, count * blocks, step, 0)


def back_heads(heads, q_aug, k_aug, k_nat, v_nat, logs, d_mine, d_recv):
    tokens = q_aug.shape[2]
    n = heads[1] - heads[0]
    outs = (sds((n, HD, tokens), f32), sds((n, tokens, HD), f32), sds((n, tokens, HD), f32))
    return kernel_call(functools.partial(back_heads_kernel, heads), outs, [pltpu.VMEM((n, HD, tokens), bf16)], 0, 7)(
        q_aug, k_aug, k_nat, v_nat, logs, d_mine, d_recv
    )


def back_kernel(
    pos, normed, w_own, qrot, krot, dq_a, dk_a, dv_a, dq_b, dk_b, dv_b, cos, sin, rows, cols, own_a, own_b, oth_a, oth_b,
    mom, vec_in,
    mine, s1, s2, s3, dn_own, dn_oth,
    dm, dm_full, freq, d_w, vec,
):
    core, band, chip, group = pos[0], pos[1], pos[2], pos[3]
    tokens = normed.shape[0]
    half = tokens // 2
    slab = half // 2
    dm_full[...] = jnp.zeros_like(dm_full)
    freq[...] = jnp.zeros_like(freq)
    for h in range(OWN_HEADS):
        c = cos[h * HALF : (h + 1) * HALF, :]
        s = sin[h * HALF : (h + 1) * HALF, :]
        na = dq_a.shape[0]
        dq, dk, dv, i = (dq_a, dk_a, dv_a, h) if h < na else (dq_b, dk_b, dv_b, h - na)
        angle = None
        for which, source, rotated in ((0, dq[i], qrot), (1, dk[i].T, krot)):
            du = source[0:HALF, :]
            dw = source[HALF:HD, :]
            u = rotated[h * HD : h * HD + HALF, :]
            w = rotated[h * HD + HALF : (h + 1) * HD, :]
            turn = dw * u - du * w
            angle = turn if angle is None else angle + turn
            at = which * OWN + h * HD
            dm[at : at + HD, :] = jnp.concatenate([du * c + dw * s, dw * c - du * s], axis=0).astype(bf16)
        at = pl.multiple_of(core * 96 + h * HALF, 32)
        freq[pl.ds(at, HALF), :] = jnp.sum(angle * rows[...], axis=1, keepdims=True)
        at = pl.multiple_of(192 + core * 96 + h * HALF, 32)
        freq[pl.ds(at, HALF), :] = jnp.sum(angle * cols[...], axis=1, keepdims=True)
        at = 2 * OWN + h * HD
        dm[at : at + HD, :] = dv[i].T.astype(bf16)
    for t in range(3):
        at = pl.multiple_of(t * D + core * OWN, 16)
        dm_full[pl.ds(at, OWN), :] = dm[t * OWN : (t + 1) * OWN, :]
    d_w[...] = dot_nn(dm[...], normed[...])
    for j in range(3):
        whole = band * 3 + j
        here = jnp.logical_and(lax.rem(whole, 4) // 2 == core, group == 0)
        at = pl.multiple_of(((whole // 4) * 2 + lax.rem(whole, 2)) * 96, 32)

        @pl.when(here)
        def _():
            d_w[pl.ds(at, 96), :] += 0.5 * mom[j * 96 : (j + 1) * 96, :]

    vec[...] = vec_in[...]
    sums = dot_nt(jnp.ones((8, tokens), bf16), dm_full[...])
    for t in range(3):
        vec[4 + t : 5 + t, :] += sums[0:1, t * D : (t + 1) * D]
    vec[13:14, :] += jnp.broadcast_to(freq[...], (D, 128)).T[0:1, :]
    for b, src in enumerate((own_a, own_b, oth_a, oth_b)):
        part = dot_tn(dm[:, b * slab : (b + 1) * slab], w_own[...])
        xhat, _ = norm_rows(src[0:slab, :].astype(f32))
        vec[0:1, :] += jnp.sum(part * xhat, axis=0, keepdims=True)
        vec[2:3, :] += jnp.sum(part, axis=0, keepdims=True)
        to, at = (dn_own, b) if b < 2 else (dn_oth, b - 2)
        to[at * slab : (at + 1) * slab, :] = part
    low = vec[...].astype(bf16)
    rows_q = mine.shape[0] - 16
    for e, ref in ((0, mine), (1, s1), (2, s2), (3, s3)):
        at = pl.multiple_of(lax.bitwise_xor(chip, e) * rows_q, 16)
        ref[0:rows_q, :] = d_w[pl.ds(at, rows_q), :].astype(ref.dtype)
        ref[rows_q : rows_q + 16, :] = low.astype(ref.dtype)


def back(pos, normed, w_own, qrot, krot, first, second, cos, sin, rows, cols, slabs, mom, vec_in):
    tokens = normed.shape[0]
    half = tokens // 2
    shape = (3 * OWN // 4 + 16, D)
    outs = (sds(shape, f32),) + (sds(shape, bf16),) * 3 + (sds((half, D), f32),) * 2
    v = pltpu.VMEM
    scratch = [
        v((3 * OWN, tokens), bf16),
        v((3 * D, tokens), bf16),
        v((D, 1), f32),
        v((3 * OWN, D), f32),
        v((16, D), f32),
    ]
    return kernel_call(back_kernel, outs, scratch, 1, 20)(
        pos, normed, w_own, qrot, krot, *first, *second, cos, sin, rows, cols, *slabs, mom, vec_in
    )


def tail_kernel(own_a, own_b, d_residual, dn_one, dn_two, gain, out_a, out_b):
    slab = out_a.shape[0]
    for b, (src, out) in enumerate(((own_a, out_a), (own_b, out_b))):
        here = slice(b * slab, (b + 1) * slab)
        xhat, rstd = norm_rows(src[0:slab, :].astype(f32))
        dx = (dn_one[here, :] + dn_two[here, :]) * gain[...]
        back_x = rstd * (
            dx - jnp.mean(dx, axis=-1, keepdims=True) - xhat * jnp.mean(dx * xhat, axis=-1, keepdims=True)
        )
        out[...] = d_residual[here, :] + back_x


def tail(own, d_residual, dn_one, dn_two, gain):
    slab = d_residual.shape[0] // 2
    outs = (sds((slab, D), f32),) * 2
    return kernel_call(tail_kernel, outs, (), 0, 6)(*own, d_residual, dn_one, dn_two, gain)


def split_low(x):
    high = x.astype(bf16)
    return high, (x - high.astype(f32)).astype(bf16)


def dot_three(a, b):
    return dot_nn(a[0], b[0]) + (dot_nn(a[0], b[1]) + dot_nn(a[1], b[0]))


def sweeps(gram):
    row = lax.broadcasted_iota(jnp.int32, (D, D), 0)
    col = lax.broadcasted_iota(jnp.int32, (D, D), 1)
    eye = (row == col).astype(f32)
    trace = jnp.sum(jnp.sum(gram * eye, axis=1, keepdims=True), axis=0, keepdims=True)
    scale = 1.0 / (jnp.sqrt(trace) + 1e-07)
    a = gram * (scale * scale)
    total = None
    for sweep in range(5):
        a2 = split_low(a)
        poly = coeff_one * eye + coeff_two * a + coeff_three * dot_three(a2, a2)
        p2 = split_low(poly)
        total = poly if total is None else dot_three(p2, split_low(total))
        if sweep < 4:
            a = dot_three(split_low(dot_three(p2, a2)), p2)
    return total * scale


def muon_big_kernel(pos, a0, a1, a2, a3, out, band_rows, big):
    chip = pos[2]
    for e, ref in enumerate((a0, a1, a2, a3)):
        for d in range(4):
            at = (e * 4 + d) * 96
            big[at : at + 96, :] = ref[d, 0:96, :]
        at = pl.multiple_of(lax.bitwise_xor(chip, e) * 96, 32)
        band_rows[pl.ds(at, 96), :] = ref[0, 0:96, :]
    out[...] = sweeps(dot_tn(big[...], big[...]))


def muon_big(pos, parts):
    outs = (sds((D, D), f32), sds((D, D), bf16))
    return kernel_call(muon_big_kernel, outs, [pltpu.VMEM((FF, D), bf16)], 1, 4)(pos, *parts)


def muon_small_kernel(pos, a0, a1, a2, a3, q0, q1, q2, q3, o0, o1, o2, o3, out, gram, rows):
    core = pos[0]
    n = q0.shape[0] - 16

    @pl.when(core == 0)
    def _():
        for e, ref in enumerate((q0, q1, q2, q3, o0, o1, o2, o3)):
            rows[e * n : (e + 1) * n, :] = ref[0:n, :]
        gram[...] = dot_tn(rows[...], rows[...])

    @pl.when(core != 0)
    def _():
        for e, ref in enumerate((a0, a1, a2, a3)):
            for d in range(4):
                at = (e * 4 + d) * 32
                rows[at : at + 32, :] = ref[d, 96:128, :]
        gram[...] = dot_tn(rows[0:512, :], rows[0:512, :])

    out[...] = sweeps(gram[...])


def muon_small(pos, parts, own_q, oth_q):
    scratch = [pltpu.VMEM((D, D), f32), pltpu.VMEM((3 * D, D), bf16)]
    return kernel_call(muon_small_kernel, sds((D, D), f32), scratch, 1, 12)(pos, *parts, *own_q, *oth_q)


def final_kernel(
    pos, one, one_oth, two, two_oth, band_mine, band_oth, a0, a1, a2, a3, q0, q1, q2, q3, o0, o1, o2, o3,
    qkv_w, proj_w, expand_w, shrink_w,
    qkv_m, qkv_new, proj_m, proj_new, expand_m, expand_new, shrink_m, shrink_new,
    proj_rows, q_mine, q_oth, q_rows,
):
    core, band, chip = pos[0], pos[1], pos[2]
    first = core == 0
    n = q0.shape[0] - 16

    def choose(when_first, a, b):
        return split_low(jnp.where(first == when_first, a[...], b[...]))

    for e, ref in enumerate((a0, a1, a2, a3)):
        at = pl.multiple_of(lax.bitwise_xor(chip, e) * 24, 8)
        proj_rows[pl.ds(at, 24), :] = ref[0, 96:128, :].astype(f32)[0:24, :]
    for e in range(4):
        at = pl.multiple_of(lax.bitwise_xor(chip, e) * n, 16)
        q_mine[pl.ds(at, n), :] = (q0, q1, q2, q3)[e][0:n, :]
        q_oth[pl.ds(at, n), :] = (o0, o1, o2, o3)[e][0:n, :]
    for j in range(3):
        whole = band * 3 + j
        at = pl.multiple_of(((whole // 4) * 2 + lax.rem(whole, 2)) * 96, 32)
        mine = lax.rem(whole, 4) // 2 == core

        @pl.when(mine)
        def _():
            q_rows[j * 96 : (j + 1) * 96, :] = q_mine[pl.ds(at, 96), :]

        @pl.when(jnp.logical_not(mine))
        def _():
            q_rows[j * 96 : (j + 1) * 96, :] = q_oth[pl.ds(at, 96), :]

    m_shrink = jnp.where(first, band_mine[...].astype(f32), band_oth[...].astype(f32))
    m_expand = jnp.where(first, band_oth[...].astype(f32), band_mine[...].astype(f32))
    t_shrink, t_expand = choose(True, one, one_oth), choose(False, one, one_oth)
    t_qkv, t_proj = choose(True, two, two_oth), choose(False, two, two_oth)
    for w, t, m, mom, new, size in (
        (qkv_w, t_qkv, q_rows[...].astype(f32), qkv_m, qkv_new, 3 * D),
        (proj_w, t_proj, proj_rows[...], proj_m, proj_new, D),
        (expand_w, t_expand, m_expand, expand_m, expand_new, FF),
    ):
        low = m.astype(bf16)
        mom[...] = m.T
        new[...] = w[...] - 0.05 * math.sqrt(size) * (dot_nt(t[0], low) + dot_nt(t[1], low))
    low = m_shrink.astype(bf16)
    shrink_m[...] = m_shrink
    shrink_new[...] = shrink_w[...] - 0.05 * math.sqrt(FF) * (dot_nn(low, t_shrink[0]) + dot_nn(low, t_shrink[1]))


def final(pos, one, one_oth, two, two_oth, band_mine, band_oth, parts, own_q, oth_q, *weights):
    outs = []
    for w in weights:
        outs += [sds(w.shape, f32)] * 2
    v = pltpu.VMEM
    scratch = [v((96, D), f32), v((3 * OWN, D), bf16), v((3 * OWN, D), bf16), v((288, D), bf16)]
    return kernel_call(final_kernel, tuple(outs), scratch, 1, 22)(
        pos, one, one_oth, two, two_oth, band_mine, band_oth, *parts, *own_q, *oth_q, *weights
    )


def flip(x, bit):
    n = lax.axis_size("batch")
    return lax.ppermute(x, "batch", [(i, i ^ bit) for i in range(n)])


def swap_bands(x, d):
    return lax.ppermute(x, "rows", [(i, i ^ d) for i in range(4)])


def moves(which):
    pairs = []
    for k in range(lax.axis_size("batch") // 2):
        for c in range(2):
            for i in range(4):
                band = (i - 2 * c - which) % 4
                pairs.append(((2 * k + i // 2) * 4 + band, (2 * k + c) * 4 + i))
    return pairs


def to_image(slabs, band):
    even = band % 2 == 0
    return [
        lax.ppermute(jnp.where(even, slabs[which], slabs[1 - which]), AXES, moves(which)) for which in range(2)
    ]


def from_image(parts, band):
    got = [lax.ppermute(parts[which], AXES, [(b, a) for a, b in moves(which)]) for which in range(2)]
    even = band % 2 == 0
    return jnp.stack([jnp.where(even, got[0], got[1]), jnp.where(even, got[1], got[0])])


def pick(x, at, axis=0):
    return lax.dynamic_index_in_dim(x, at, axis, keepdims=False)


def other_chips(x):
    bit = 8
    while bit < lax.axis_size("batch"):
        x = x + flip(x.astype(f32), bit).astype(x.dtype)
        bit *= 2
    return x


def over_chips(x):
    return [flip(x, 2 * e) for e in range(1, 4)]


def over_bands(x):
    return [swap_bands(x, d) for d in range(1, 4)]


def local(
    patches,
    cotangent,
    heights,
    widths,
    qkv_weight,
    qkv_moment,
    proj_weight,
    proj_moment,
    expand_weight,
    expand_moment,
    shrink_weight,
    shrink_moment,
    norm_gains,
    gains_moment,
    all_biases,
    biases_moment,
    frequencies,
    freq_moment,
):
    images, band_rows, grid_w, _ = patches.shape
    slab = band_rows * grid_w
    batch = lax.axis_index("batch")
    band = lax.axis_index("rows")
    core = batch % 2
    chip = (batch // 2) % 4
    first = core == 0
    group = batch // 2
    pos = jnp.stack([core, band, chip, group]).astype(jnp.int32)

    sizes = jnp.stack([heights, widths], axis=1).astype(bf16)
    size_rows = jnp.concatenate([sizes, jnp.zeros((images, 14), bf16)], axis=1)
    with_size = jnp.concatenate(
        [patches.reshape(images, slab, D), jnp.broadcast_to(size_rows[:, :, None], (images, 16, D))], axis=1
    )
    own = to_image(with_size, band)
    oth = [flip(x, 1) for x in own]
    start = pick(pick(jnp.array([[0, 2, 4, 0], [4, 0, 0, 2]], jnp.int32), core), band)
    count = pick(pick(jnp.array([[4, 4, 2, 2], [2, 2, 4, 4]], jnp.int32), core), band)
    qkv_at = 48 * (start + jnp.minimum(chip, count - 1))
    piece = 2 * chip + core
    proj_at = 16 * jnp.where(piece < 6, piece, 0)
    shard16 = jnp.concatenate(
        [
            lax.dynamic_slice_in_dim(qkv_weight.T.astype(bf16), qkv_at, 48, 0),
            lax.dynamic_slice_in_dim(proj_weight.T.astype(bf16), proj_at, 16, 0),
            lax.dynamic_slice_in_dim(expand_weight.T.astype(bf16), piece * 48, 48, 0),
            lax.dynamic_slice_in_dim(shrink_weight.astype(bf16), piece * 48, 48, 0),
        ]
    )
    shards = jnp.stack([shard16] + over_bands(shard16))
    qkv_own = shards[:, 0:48]
    w_qkv = [qkv_own] + over_chips(qkv_own)
    rest_own = shards[:, 48:160]
    w_rest = [rest_own] + over_chips(rest_own)
    w_rest_oth = [flip(x, 1) for x in w_rest]
    cot = to_image(cotangent.reshape(images, slab, D), band)

    slots = jnp.stack([2 * core, 2 * core + 1, 2 - 2 * core, 3 - 2 * core])
    slot_band = (band - slots) % 4
    rows_one = slot_band[:, None] * band_rows + jnp.arange(band_rows)[None, :]
    rows_tok = jnp.repeat(rows_one.reshape(-1), grid_w).astype(f32)
    cols_tok = jnp.tile(jnp.arange(grid_w), 4 * band_rows).astype(f32)
    row_col = jnp.stack([rows_tok, cols_tok], axis=1)[: 2 * slab]
    freq_own = lax.dynamic_slice_in_dim(frequencies, core * 96, 96, 1)
    angle = freq_own[0][:, None] * rows_tok[None, :] + freq_own[1][:, None] * cols_tok[None, :]
    cos, sin = jnp.cos(angle), jnp.sin(angle)
    rows_tok, cols_tok = rows_tok[None, :], cols_tok[None, :]

    gain_one, gain_two = norm_gains[0][None, :], norm_gains[1][None, :]
    shift_one, shift_two = all_biases[0:D][None, :], all_biases[D : 2 * D][None, :]
    qkv_bias = all_biases[2 * D : 5 * D].reshape(3, 2, OWN)
    bias_own = pick(qkv_bias, core, 1).reshape(3 * OWN, 1)
    proj_bias = all_biases[5 * D : 6 * D][None, :]
    expand_bias = all_biases[6 * D : 6 * D + FF].reshape(4, 1, D)
    shrink_bias = all_biases[6 * D + FF :][None, :]

    mom_s = pick(shrink_moment.reshape(4, 96, D), chip)
    mom_e = pick(expand_moment.T.reshape(4, 96, D), chip)
    mom_p = pick(proj_moment.T.reshape(4, 24, D), chip)
    mom_big = jnp.concatenate([jnp.where(first, mom_s, mom_e), mom_p, jnp.zeros((8, D), f32)])
    n_bias = all_biases.shape[0]

    def placed(shape, part, axis):
        return lax.dynamic_update_slice_in_dim(
            jnp.zeros(shape, f32), part, band * (shape[axis] // 4), axis
        ).reshape(-1)

    vec_mom = jnp.concatenate(
        [
            placed((2, D), gains_moment, 1),
            placed((n_bias,), biases_moment, 0),
            placed((2, H * HALF), freq_moment, 1),
            jnp.zeros((2 * D,), f32),
        ]
    ).reshape(16, D)
    vec_mom = jnp.where(batch == 0, 0.5 * vec_mom, 0.0)
    qkv_mom = qkv_moment.T

    normed, w_own, qrot, krot, q_aug, k_aug, k_nat, v_nat, logs, o_own, o_oth = front(
        pos, own + oth, w_qkv, bias_own, gain_one, shift_one, cos, sin, rows_tok, cols_tok
    )
    o_recv = flip(o_oth, 1)
    block_own, d_residual, d_mine, d_send, keep, send, vec_mid = middle(
        pos, own, cot, row_col, (o_own, o_recv), w_rest, w_rest_oth, gain_two, shift_two, proj_bias, expand_bias, shrink_bias
    )
    d_recv = flip(d_send, 1)
    heads_args = (q_aug, k_aug, k_nat, v_nat, logs, d_mine, d_recv)
    head_a = back_heads((0, 1), *heads_args)
    mine_big, *to_chips = merge(pos, keep, flip(send, 1))
    k_aug, to_chips = lax.optimization_barrier((k_aug, to_chips))
    from_chips = [flip(x, 2 * e) for e, x in zip((1, 2, 3), to_chips)]
    head_b = back_heads((1, 3), q_aug, k_aug, *heads_args[2:])
    mine_q, s1, s2, s3, dn_own, dn_oth = back(
        pos, normed, w_own, qrot, krot, head_a, head_b, cos, sin, rows_tok, cols_tok, own + oth, qkv_mom, vec_mid + vec_mom
    )
    dn_recv = flip(dn_oth, 1)
    q_chips = [flip(x, 2 * e) for e, x in zip((1, 2, 3), (s1, s2, s3))]

    mine_big = other_chips(mine_big)
    own_big, *to_bands = bands(pos, mine_big, from_chips)
    from_bands = [swap_bands(x, d) for d, x in zip((1, 2, 3), to_bands)]
    patch_own = tail(own, d_residual, dn_own, dn_recv, gain_one)

    q_low = other_chips(sum_low(mine_q, q_chips))
    q_piece = sum_low(q_low, over_bands(q_low))
    own_q = [q_piece] + over_chips(q_piece)
    oth_q = [flip(x, 1) for x in own_q]

    big_piece = piece_sum(own_big, from_bands, mom_big)
    big_bands = jnp.stack([big_piece] + over_bands(big_piece))
    big_all = [big_bands] + over_chips(big_bands)

    one, band_mine = muon_big(pos, big_all)
    one_oth, band_oth = flip(one, 1), flip(band_mine, 1)
    two = muon_small(pos, big_all, own_q, oth_q)
    two_oth = flip(two, 1)
    new = final(
        pos, one, one_oth, two, two_oth, band_mine, band_oth, big_all, own_q, oth_q,
        qkv_weight, proj_weight, expand_weight, shrink_weight,
    )

    block_out = from_image([block_own[:slab], block_own[slab:]], band).reshape(images, band_rows, grid_w, D)
    patch_grad = from_image(patch_own, band).reshape(images, band_rows, grid_w, D)

    vec = (own_q[0][-16:].astype(f32) + oth_q[0][-16:].astype(f32)).reshape(-1)

    def vector_step(values, new, axis):
        stepped = values - 0.2 * new * lax.rsqrt(jnp.mean(new * new) + 1e-06)
        size_one = new.shape[axis] // 4
        return (
            lax.dynamic_slice_in_dim(new, band * size_one, size_one, axis),
            lax.dynamic_slice_in_dim(stepped, band * size_one, size_one, axis),
        )

    vectors = (
        vector_step(norm_gains, vec[: 2 * D].reshape(2, D), 1)
        + vector_step(all_biases, vec[2 * D : 2 * D + n_bias], 0)
        + vector_step(frequencies, vec[2 * D + n_bias : 2 * D + n_bias + H * HD].reshape(2, H * HALF), 1)
    )
    return (block_out, patch_grad) + tuple(new) + vectors


def solution(mesh):
    image = P("batch", "rows", None, None)
    cols, rows = P(None, "rows"), P("rows", None)
    return jax.shard_map(
        local,
        mesh=mesh,
        in_specs=(
            image, image, P("batch"), P("batch"), cols, cols, cols, cols, cols, cols, rows, rows,
            P(), cols, P(), P("rows"), P(), cols,
        ),
        out_specs=(
            image, image, cols, cols, cols, cols, cols, cols, rows, rows, cols, cols, P("rows"), P("rows"), cols, cols,
        ),
        check_vma=False,
    )
```

time: 1540 us -> 262 us (0.17)
  waiting for transfers between devices: 647 us -> 48.3 us
  local copies, waits for them, and re-layouts: 408 us -> 22.7 us
  matrix products: 221 us -> 0 us
  blocking collectives: 94.9 us -> 0 us
  Pallas kernels: 0 us -> 94.6 us
  starting transfers between devices: 1.14 us -> 74 us
  loops' own time: 71.1 us -> 0 us
  other arithmetic: 58.9 us -> 13.2 us
  between operations: 20.9 us -> 4.84 us
    psum x6 -> x0, waiting for transfers between devices: 555 us -> none  [the longest x5 394 us: local(): lax.psum((partial_grams[0], partial_grams[1], partial_grams[2], partial_g...]
    unnamed x258 -> x65, local copies, waits for them, and re-layouts: 328 us -> 12.5 us
    dot_general x156 -> x0, matrix products: 221 us -> none  [the longest x20 39.2 us: local(): jnp.einsum('ik,jk->ij', column_block, column_block, precision=highest)]
    pallas_call x0 -> x14, Pallas kernels: none -> 94.6 us  [the longest x2 17.9 us: back_heads(): kernel_call(functools.partial(back_heads_kernel, heads), outs, [pltpu.VME...]
    ppermute x0 -> x55, starting transfers between devices: none -> 74 us  [the longest x35 40 us: flip(): return lax.ppermute(x, 'batch', [(i, i ^ bit) for i in range(n)])]
    another operation x2 -> x0, loops' own time: 71.1 us -> none  [the longest x1 47.2 us: local(): lax.map(query_and_keys, jnp.arange(item_count, dtype=jnp.int32))]
    psum x2 -> x0, blocking collectives: 53 us -> none  [the longest x1 42.6 us: local(): lax.psum((d_qkv, d_proj, d_expand, d_shrink, gain_grad, bias_grad, d_freq...]
    all_gather x4 -> x0, waiting for transfers between devices: 49.3 us -> none  [the longest x1 36.3 us: local(): lax.all_gather(values16, 'rows', axis=1, tiled=True)]
  transfers between devices with their start and end apart: 12 -> 55, of which waited for: 9 -> 16; matrix products, arithmetic and copies ran while one was open for 24% -> 7% of each run, Pallas kernels for 0% -> 21%
where the time goes in v1:
time: 262 us; the launch traced here: 258 us
  Pallas kernels  94.6 us (36%)
  starting transfers between devices  74 us (28%)
  waiting for transfers between devices  48.3 us (18%)
  local copies, waits for them, and re-layouts  22.7 us (9%)
  other arithmetic  13.2 us (5%)
  between operations  4.84 us (2%)
    ppermute x35, starting transfers between devices, flip(): return lax.ppermute(x, 'batch', [(i, i ^ bit) for i in range(n)])  40 us
    ppermute x35, waiting for transfers between devices, flip(): return lax.ppermute(x, 'batch', [(i, i ^ bit) for i in range(n)])  24 us
    ppermute x12, waiting for transfers between devices, swap_bands(): return lax.ppermute(x, 'rows', [(i, i ^ d) for i in range(4)])  23.8 us
    ppermute x12, starting transfers between devices, swap_bands(): return lax.ppermute(x, 'rows', [(i, i ^ d) for i in range(4)])  22.9 us
    pallas_call x2, Pallas kernels, back_heads(): kernel_call(functools.partial(back_heads_kernel, heads), outs, [pltpu.VME...  17.9 us
    pallas_call x1, Pallas kernels, muon_small(): kernel_call(muon_small_kernel, sds((D, D), f32), scratch, 1, 12)  14.7 us
    pallas_call x1, Pallas kernels, front(): kernel_call(front_kernel, outs, scratch, 1, 15)  14.6 us
    pallas_call x1, Pallas kernels, muon_big(): kernel_call(muon_big_kernel, outs, [pltpu.VMEM((FF, D), bf16)], 1, 4)  13.9 us
  transfers between devices with their start and end apart: 55, of which 16 were waited for; matrix products, arithmetic and copies ran while one was open for 7% of the time, Pallas kernels for 21%

profile of v1, /device:TPU:0, one launch (start us, length us, event | category | flops | bytes accessed | tf_op | source)
XLA Modules:
  0.0 257.6 jit_solution(9838042096711897899)
XLA Ops:
  8.4 3.1 %collective-permute-start.6 = (bf16[160,384]{1,0:T(8,128)(2,1)S(1)}, bf16[160,384]{1,0:T(8,128)(2,1)S(1)}, u32[]{:S(2)}, u32[]{:S(2)}) collective-permute-start(bf16[160,384]{1,0:T(8,128)(2,1)S(1)} %get-tuple-element.191), channel_id=1, source_target_pairs={{0,1},{1,0},{2,3},{3,2},{4,5},{5,4},{6,7},{7,6},{8,9},{9,8},{10,11... | collective-permute-start | bytes 368648 | tf_op jit(solution)/shard_map/ppermute | solution.py:634
  11.5 2.6 %collective-permute-start.7 = (bf16[160,384]{1,0:T(8,128)(2,1)S(1)}, bf16[160,384]{1,0:T(8,128)(2,1)S(1)}, u32[]{:S(2)}, u32[]{:S(2)}) collective-permute-start(bf16[160,384]{1,0:T(8,128)(2,1)S(1)} %get-tuple-element.191), channel_id=1, source_target_pairs={{0,2},{1,3},{2,0},{3,1},{4,6},{5,7},{6,4},{7,5},{8,10},{9,11},{10,... | collective-permute-start | bytes 368648 | tf_op jit(solution)/shard_map/ppermute | solution.py:634
  18.8 5.4 %collective-permute-done.7 = bf16[160,384]{1,0:T(8,128)(2,1)S(1)} collective-permute-done((bf16[160,384]{1,0:T(8,128)(2,1)S(1)}, bf16[160,384]{1,0:T(8,128)(2,1)S(1)}, u32[]{:S(2)}, u32[]{:S(2)}) %collective-permute-start.7) | collective-permute-done | bytes 122912 | tf_op jit(solution)/shard_map/ppermute | solution.py:634
  31.7 2.0 collective-permute-done.10.w2
  33.7 2.4 collective-permute-start.15
  36.0 2.3 fusion
  38.3 6.4 %collective-permute-start.4 = (bf16[272,384]{1,0:T(8,128)(2,1)S(1)}, bf16[272,384]{1,0:T(8,128)(2,1)S(1)}, u32[]{:S(2)}, u32[]{:S(2)}) collective-permute-start(bf16[272,384]{1,0:T(8,128)(2,1)S(1)} %collective-permute-done.own_a), channel_id=1, source_target_pairs={{0,4},{4,0},{8,12},{12,8},{16,20},{20,16},{24,28},{28,24},{1,5},{5... | collective-permute-start | bytes 626696 | tf_op jit(solution)/shard_map/ppermute | solution.py:630
  46.2 2.1 collective-permute-start.16
  48.8 2.1 collective-permute-start.19
  52.3 14.6 %shard_map.315 = (bf16[1024,384]{1,0:T(8,128)(2,1)}, bf16[576,384]{1,0:T(8,128)(2,1)}, f32[192,1024]{1,0:T(8,128)}, f32[192,1024]{1,0:T(8,128)}, bf16[3,80,1024]...) custom-call(s32[4]{0:T(128)S(1)} %pad_add_fusion.pos, ...), custom_call_target="tpu_custom_call" | custom-call | tf_op jit(solution)/shard_map/pallas_call | solution.py:162
  68.5 12.8 %shard_map.316 = (bf16[512,384]{1,0:T(8,128)(2,1)}, f32[512,384]{1,0:T(8,128)}, bf16[192,512]{1,0:T(8,128)(2,1)S(1)}, bf16[192,512]{1,0:T(8,128)(2,1)S(1)}, f32[...) custom-call(s32[4]{0:T(128)S(1)} %pad_add_fusion.pos, ...), custom_call_target="tpu_custom_call" | custom-call | tf_op jit(solution)/shard_map/pallas_call | solution.py:292
  82.5 2.2 collective-permute-done.22.d_recv
  84.8 6.5 %shard_map.317 = (f32[1,64,1024]{2,1,0:T(8,128)S(1)}, f32[1,1024,64]{2,1,0:T(8,128)}, f32[1,1024,64]{2,1,0:T(8,128)}) custom-call(bf16[3,80,1024]{2,1,0:T(8,128)(2,1)S(1)} %copy-done.7, bf16[3,80,1024]{2,1,0:T(8,128)(2,1)S(1)} %copy-done.8, bf16[3,1024,80]{2,1,0:T(8,128)(2,1)} %get-tuple-element.80.k_nat, bf16[3,1024,64]{2,1,0:T(8,128)(2,1)} %get-tuple-element.81.v_nat, ...), custom_call_target="tpu_custom_call" | custom-call | tf_op jit(solution)/shard_map/pallas_call | solution.py:391
  91.3 3.6 %shard_map.318 = (f32[4,128,384]{2,1,0:T(8,128)S(1)}, bf16[4,128,384]{2,1,0:T(8,128)(2,1)}, bf16[4,128,384]{2,1,0:T(8,128)(2,1)}, bf16[4,128,384]{2,1,0:T(8,128)(2,1)S(1)}) custom-call(s32[4]{0:T(128)S(1)} %pad_add_fusion.pos, f32[4,4,128,384]{3,2,1,0:T(8,128)} %get-tuple-element.88.keep, bf16[4,4,128,384]{3,2,1,0:T(8,128)(2,1)} %collective-permute-done.23.recv), custom_call_target="tpu_custom_call" | custom-call | tf_op jit(solution)/shard_map/pallas_call | solution.py:313
  94.9 11.3 %shard_map.319 = (f32[2,64,1024]{2,1,0:T(8,128)S(1)}, f32[2,1024,64]{2,1,0:T(8,128)}, f32[2,1024,64]{2,1,0:T(8,128)}) custom-call(bf16[3,80,1024]{2,1,0:T(8,128)(2,1)S(1)} %copy-done.7, bf16[3,80,1024]{2,1,0:T(8,128)(2,1)S(1)} %copy-done.8, bf16[3,1024,80]{2,1,0:T(8,128)(2,1)} %get-tuple-element.80.k_nat, bf16[3,1024,64]{2,1,0:T(8,128)(2,1)} %get-tuple-element.81.v_nat, ...), custom_call_target="tpu_custom_call" | custom-call | tf_op jit(solution)/shard_map/pallas_call | solution.py:391
  107.0 7.3 %shard_map.320 = (f32[160,384]{1,0:T(8,128)S(1)}, bf16[160,384]{1,0:T(8,128)(2,1)S(1)}, bf16[160,384]{1,0:T(8,128)(2,1)S(1)}, bf16[160,384]{1,0:T(8,128)(2,1)S(1...) custom-call(s32[4]{0:T(128)S(1)} %pad_add_fusion.pos, bf16[1024,384]{1,0:T(8,128)(2,1)} %get-tuple-element.74.normed, ...), custom_call_target="tpu_custom_call" | custom-call | tf_op jit(solution)/shard_map/pallas_call | solution.py:475
  124.0 7.3 %collective-permute-start.43 = (bf16[160,384]{1,0:T(8,128)(2,1)S(1)}, bf16[160,384]{1,0:T(8,128)(2,1)S(1)}, u32[]{:S(2)}, u32[]{:S(2)}) collective-permute-start(bf16[160,384]{1,0:T(8,128)(2,1)S(1)} %shard_map.325.own), channel_id=1, source_target_pairs={{0,1},{1,0},{2,3},{3,2},{4,5},{5,4},{6,7},{7,6},{8,9},{9,8},{10,11... | collective-permute-start | bytes 368648 | tf_op jit(solution)/shard_map/ppermute | solution.py:634
  135.5 3.5 %collective-permute-start.21 = (bf16[256,384]{1,0:T(8,128)(2,1)S(1)}, bf16[256,384]{1,0:T(8,128)(2,1)S(1)}, u32[]{:S(2)}, u32[]{:S(2)}) collective-permute-start(bf16[256,384]{1,0:T(8,128)(2,1)S(1)} %get-tuple-element.187), channel_id=1, source_target_pairs={{0,3},{1,0},{2,5},{3,6},{4,1},{5,2},{6,7},{7,4},{8,11},{9,8},{10,1... | collective-permute-start | bytes 589832 | tf_op jit(solution)/shard_map/ppermute | solution.py:655
  139.0 6.1 %collective-permute-done.44.r2 = bf16[160,384]{1,0:T(8,128)(2,1)S(1)} collective-permute-done((bf16[160,384]{1,0:T(8,128)(2,1)S(1)}, bf16[160,384]{1,0:T(8,128)(2,1)S(1)}, u32[]{:S(2)}, u32[]{:S(2)}) %collective-permute-start.44) | collective-permute-done | bytes 122912 | tf_op jit(solution)/shard_map/ppermute | solution.py:634
  148.0 3.9 %collective-permute-start.24 = (f32[512,384]{1,0:T(8,128)S(1)}, f32[512,384]{1,0:T(8,128)S(1)}, u32[]{:S(2)}, u32[]{:S(2)}) collective-permute-start(f32[512,384]{1,0:T(8,128)S(1)} %copy-done.27), channel_id=1, source_target_pairs={{0,4},{4,0},{8,12},{12,8},{16,20},{20,16},{24,28},{28,24},{1,5},{5... | collective-permute-start | bytes 2359304 | tf_op jit(solution)/shard_map/ppermute | solution.py:630
  152.9 9.3 %collective-permute-done.28.r2 = bf16[4,128,384]{2,1,0:T(8,128)(2,1)S(1)} collective-permute-done((bf16[4,128,384]{2,1,0:T(8,128)(2,1)}, bf16[4,128,384]{2,1,0:T(8,128)(2,1)S(1)}, u32[]{:S(2)}, u32[]{:S(2)}) %collective-permute-start.28) | collective-permute-done | bytes 393248 | tf_op jit(solution)/shard_map/ppermute | solution.py:630
  168.2 2.9 %collective-permute-start.32 = (bf16[128,384]{1,0:T(8,128)(2,1)S(1)}, bf16[128,384]{1,0:T(8,128)(2,1)S(1)}, u32[]{:S(2)}, u32[]{:S(2)}) collective-permute-start(bf16[128,384]{1,0:T(8,128)(2,1)S(1)} %get-tuple-element.109), channel_id=1, source_target_pairs={{0,3},{1,2},{2,1},{3,0},{4,7},{5,6},{6,5},{7,4},{8,11},{9,10},{10,... | collective-permute-start | bytes 294920 | tf_op jit(solution)/shard_map/ppermute | solution.py:634
  171.2 4.4 %collective-permute-done.31.r2 = bf16[128,384]{1,0:T(8,128)(2,1)S(1)} collective-permute-done((bf16[128,384]{1,0:T(8,128)(2,1)S(1)}, bf16[128,384]{1,0:T(8,128)(2,1)S(1)}, u32[]{:S(2)}, u32[]{:S(2)}) %collective-permute-start.31) | collective-permute-done | bytes 98336 | tf_op jit(solution)/shard_map/ppermute | solution.py:634
  181.9 5.2 %collective-permute-done.34 = bf16[128,384]{1,0:T(8,128)(2,1)S(1)} collective-permute-done((bf16[128,384]{1,0:T(8,128)(2,1)S(1)}, bf16[128,384]{1,0:T(8,128)(2,1)S(1)}, u32[]{:S(2)}, u32[]{:S(2)}) %collective-permute-start.34) | collective-permute-done | bytes 98336 | tf_op jit(solution)/shard_map/ppermute | solution.py:634
  191.4 2.7 %shard_map.321 = (f32[256,384]{1,0:T(8,128)}, f32[256,384]{1,0:T(8,128)}) custom-call(bf16[272,384]{1,0:T(8,128)(2,1)S(1)} %collective-permute-done.own_a, bf16[272,384]{1,0:T(8,128)(2,1)S(1)} %collective-permute-done.1.own_b, f32[512,384]{1,0:T(8,128)S(1)} %copy-done.10, f32[512,384]{1,0:T(8,128)} %get-tuple-element.98.dn_one, f32[512,384]{1,0:T(8,128)} %copy-done.13, ...), custom_call_target="tpu_custom_call" | custom-call | tf_op jit(solution)/shard_map/pallas_call | solution.py:495
  194.1 4.5 %collective-permute-start.25 = (f32[256,384]{1,0:T(8,128)}, f32[256,384]{1,0:T(8,128)}, u32[]{:S(2)}, u32[]{:S(2)}) collective-permute-start(f32[256,384]{1,0:T(8,128)} %get-tuple-element.100), channel_id=1, source_target_pairs={{0,0},{1,1},{2,6},{3,7},{4,2},{5,3},{6,4},{7,5},{8,8},{9,9},{10,14... | collective-permute-start | bytes 1179656 | tf_op jit(solution)/shard_map/ppermute | solution.py:655
  202.0 4.6 %collective-permute-done.37.a2 = bf16[4,128,384]{2,1,0:T(8,128)(2,1)S(1)} collective-permute-done((bf16[4,128,384]{2,1,0:T(8,128)(2,1)S(1)}, bf16[4,128,384]{2,1,0:T(8,128)(2,1)S(1)}, u32[]{:S(2)}, u32[]{:S(2)}) %collective-permute-start.37) | collective-permute-done | bytes 393248 | tf_op jit(solution)/shard_map/ppermute | solution.py:630
  209.2 14.7 %shard_map.327.two = f32[384,384]{1,0:T(8,128)} custom-call(s32[4]{0:T(128)S(1)} %pad_add_fusion.pos, bf16[4,128,384]{2,1,0:T(8,128)(2,1)S(1)} %pad_maximum_fusion.2.a0, bf16[4,128,384]{2,1,0:T(8,128)(2,1)S(1)} %collective-permute-done.36.a1, bf16[4,128,384]{2,1,0:T(8,128)(2,1)} %copy-done.3, bf16[4,128,384]{2,1,0:T(8,128)(2,1)} %copy-done.5, ...), custom_call_target="tpu_custom_call" | custom-call | tf_op jit(solution)/shard_map/pallas_call | solution.py:564
  225.9 13.9 %shard_map.324 = (f32[384,384]{1,0:T(8,128)}, bf16[384,384]{1,0:T(8,128)(2,1)S(1)}) custom-call(s32[4]{0:T(128)S(1)} %pad_add_fusion.pos, bf16[4,128,384]{2,1,0:T(8,128)(2,1)S(1)} %pad_maximum_fusion.2.a0, bf16[4,128,384]{2,1,0:T(8,128)(2,1)S(1)} %collective-permute-done.36.a1, bf16[4,128,384]{2,1,0:T(8,128)(2,1)S(1)} %copy-done.4, ...), custom_call_target="tpu_custom_call" | custom-call | tf_op jit(solution)/shard_map/pallas_call | solution.py:538
  246.2 5.6 %shard_map.328 = (f32[384,288]{1,0:T(8,128)}, f32[384,288]{1,0:T(8,128)}, f32[384,96]{1,0:T(8,128)S(1)}, f32[384,96]{1,0:T(8,128)S(1)}, f32[384,384]{1,0:T(8,128...) custom-call(s32[4]{0:T(128)S(1)} %pad_add_fusion.pos, f32[384,384]{1,0:T(8,128)} %get-tuple-element.110.one, ...), custom_call_target="tpu_custom_call" | custom-call | tf_op jit(solution)/shard_map/pallas_call | solution.py:623
  251.8 2.0 copy.64
  253.8 2.0 copy.65
  (233 shorter events, 73.3 us)
Async XLA Ops:
  11.5 12.7 %collective-permute-start.7 = (bf16[160,384]{1,0:T(8,128)(2,1)S(1)}, bf16[160,384]{1,0:T(8,128)(2,1)S(1)}, u32[]{:S(2)}, u32[]{:S(2)}) collective-permute-start(bf16[160,384]{1,0:T(8,128)(2,1)S(1)} %get-tuple-element.191), channel_id=1, source_target_pairs={{0,2},{1,3},{2,0},{3,1},{4,6},{5,7},{6,4},{7,5},{8,10},{9,11},{10,... | collective-permute-start | bytes 368648 | tf_op jit(solution)/shard_map/ppermute | solution.py:634
  16.9 13.3 %collective-permute-start.1 = (bf16[272,384]{1,0:T(8,128)(2,1)S(1)}, bf16[272,384]{1,0:T(8,128)(2,1)S(1)}, u32[]{:S(2)}, u32[]{:S(2)}) collective-permute-start(bf16[272,384]{1,0:T(8,128)(2,1)S(1)} %get-tuple-element.182), channel_id=1, source_target_pairs={{3,0},{0,1},{5,2},{6,3},{1,4},{2,5},{7,6},{4,7},{11,8},{8,9},{13,1... | collective-permute-start | bytes 626696 | tf_op jit(solution)/shard_map/ppermute | solution.py:650
  26.1 12.2 %collective-permute-start.11 = (bf16[4,48,384]{2,1,0:T(8,128)(2,1)S(1)}, bf16[4,48,384]{2,1,0:T(8,128)(2,1)S(1)}, u32[]{:S(2)}, u32[]{:S(2)}) collective-permute-start(bf16[4,48,384]{2,1,0:T(8,128)(2,1)S(1)} %pad_maximum_fusion.7.w0), channel_id=1, source_target_pairs={{0,24},{4,28},{8,16},{12,20},{16,8},{20,12},{24,0},{28,4},{1,25},{... | collective-permute-start | bytes 442376 | tf_op jit(solution)/shard_map/ppermute | solution.py:630
  27.6 17.1 %collective-permute-start.9 = (bf16[4,48,384]{2,1,0:T(8,128)(2,1)S(1)}, bf16[4,48,384]{2,1,0:T(8,128)(2,1)S(1)}, u32[]{:S(2)}, u32[]{:S(2)}) collective-permute-start(bf16[4,48,384]{2,1,0:T(8,128)(2,1)S(1)} %pad_maximum_fusion.7.w0), channel_id=1, source_target_pairs={{0,8},{4,12},{8,0},{12,4},{16,24},{20,28},{24,16},{28,20},{1,9},{5... | collective-permute-start | bytes 442376 | tf_op jit(solution)/shard_map/ppermute | solution.py:630
  28.2 20.1 %collective-permute-start.13 = (bf16[4,112,384]{2,1,0:T(8,128)(2,1)S(1)}, bf16[4,112,384]{2,1,0:T(8,128)(2,1)}, u32[]{:S(2)}, u32[]{:S(2)}) collective-permute-start(bf16[4,112,384]{2,1,0:T(8,128)(2,1)S(1)} %pad_maximum_fusion.3.m0), channel_id=1, source_target_pairs={{0,8},{4,12},{8,0},{12,4},{16,24},{20,28},{24,16},{28,20},{1,9},{5... | collective-permute-start | bytes 1032200 | tf_op jit(solution)/shard_map/ppermute | solution.py:630
  30.2 18.2 %collective-permute-start.14 = (bf16[4,112,384]{2,1,0:T(8,128)(2,1)S(1)}, bf16[4,112,384]{2,1,0:T(8,128)(2,1)}, u32[]{:S(2)}, u32[]{:S(2)}) collective-permute-start(bf16[4,112,384]{2,1,0:T(8,128)(2,1)S(1)} %pad_maximum_fusion.3.m0), channel_id=1, source_target_pairs={{0,16},{4,20},{8,24},{12,28},{16,0},{20,4},{24,8},{28,12},{1,17},{... | collective-permute-start | bytes 1032200 | tf_op jit(solution)/shard_map/ppermute | solution.py:630
  33.7 15.2 %collective-permute-start.15 = (bf16[4,112,384]{2,1,0:T(8,128)(2,1)S(1)}, bf16[4,112,384]{2,1,0:T(8,128)(2,1)}, u32[]{:S(2)}, u32[]{:S(2)}) collective-permute-start(bf16[4,112,384]{2,1,0:T(8,128)(2,1)S(1)} %pad_maximum_fusion.3.m0), channel_id=1, source_target_pairs={{0,24},{4,28},{8,16},{12,20},{16,8},{20,12},{24,0},{28,4},{1,25},{... | collective-permute-start | bytes 1032200 | tf_op jit(solution)/shard_map/ppermute | solution.py:630
  45.8 21.1 %collective-permute-start.3 = (bf16[256,384]{1,0:T(8,128)(2,1)S(1)}, bf16[256,384]{1,0:T(8,128)(2,1)S(1)}, u32[]{:S(2)}, u32[]{:S(2)}) collective-permute-start(bf16[256,384]{1,0:T(8,128)(2,1)S(1)} %bitcast.72), channel_id=1, source_target_pairs={{3,0},{0,1},{5,2},{6,3},{1,4},{2,5},{7,6},{4,7},{11,8},{8,9},{13,1... | collective-permute-start | bytes 589832 | tf_op jit(solution)/shard_map/ppermute | solution.py:650
  46.2 21.2 %collective-permute-start.16 = (bf16[4,112,384]{2,1,0:T(8,128)(2,1)S(1)}, bf16[4,112,384]{2,1,0:T(8,128)(2,1)}, u32[]{:S(2)}, u32[]{:S(2)}) collective-permute-start(bf16[4,112,384]{2,1,0:T(8,128)(2,1)S(1)} %pad_maximum_fusion.3.m0), channel_id=1, source_target_pairs={{0,4},{4,0},{8,12},{12,8},{16,20},{20,16},{24,28},{28,24},{1,5},{5... | collective-permute-start | bytes 1032200 | tf_op jit(solution)/shard_map/ppermute | solution.py:630
  48.3 20.1 %collective-permute-start.17 = (bf16[4,112,384]{2,1,0:T(8,128)(2,1)}, bf16[4,112,384]{2,1,0:T(8,128)(2,1)}, u32[]{:S(2)}, u32[]{:S(2)}) collective-permute-start(bf16[4,112,384]{2,1,0:T(8,128)(2,1)} %collective-permute-done.13.m1), channel_id=1, source_target_pairs={{0,4},{4,0},{8,12},{12,8},{16,20},{20,16},{24,28},{28,24},{1,5},{5... | collective-permute-start | bytes 1032200 | tf_op jit(solution)/shard_map/ppermute | solution.py:630
  48.4 20.0 %collective-permute-start.18 = (bf16[4,112,384]{2,1,0:T(8,128)(2,1)}, bf16[4,112,384]{2,1,0:T(8,128)(2,1)}, u32[]{:S(2)}, u32[]{:S(2)}) collective-permute-start(bf16[4,112,384]{2,1,0:T(8,128)(2,1)} %collective-permute-done.14.m2), channel_id=1, source_target_pairs={{0,4},{4,0},{8,12},{12,8},{16,20},{20,16},{24,28},{28,24},{1,5},{5... | collective-permute-start | bytes 1032200 | tf_op jit(solution)/shard_map/ppermute | solution.py:630
  48.8 19.5 %collective-permute-start.19 = (bf16[4,112,384]{2,1,0:T(8,128)(2,1)}, bf16[4,112,384]{2,1,0:T(8,128)(2,1)}, u32[]{:S(2)}, u32[]{:S(2)}) collective-permute-start(bf16[4,112,384]{2,1,0:T(8,128)(2,1)} %collective-permute-done.15.m3), channel_id=1, source_target_pairs={{0,4},{4,0},{8,12},{12,8},{16,20},{20,16},{24,28},{28,24},{1,5},{5... | collective-permute-start | bytes 1032200 | tf_op jit(solution)/shard_map/ppermute | solution.py:630
  120.4 31.6 %collective-permute-start.27 = (bf16[4,128,384]{2,1,0:T(8,128)(2,1)}, bf16[4,128,384]{2,1,0:T(8,128)(2,1)S(1)}, u32[]{:S(2)}, u32[]{:S(2)}) collective-permute-start(bf16[4,128,384]{2,1,0:T(8,128)(2,1)} %get-tuple-element.103), channel_id=1, source_target_pairs={{0,8},{4,12},{8,0},{12,4},{16,24},{20,28},{24,16},{28,20},{1,9},{5... | collective-permute-start | bytes 1179656 | tf_op jit(solution)/shard_map/ppermute | solution.py:630
  131.3 13.8 %collective-permute-start.44 = (bf16[160,384]{1,0:T(8,128)(2,1)S(1)}, bf16[160,384]{1,0:T(8,128)(2,1)S(1)}, u32[]{:S(2)}, u32[]{:S(2)}) collective-permute-start(bf16[160,384]{1,0:T(8,128)(2,1)S(1)} %shard_map.325.own), channel_id=1, source_target_pairs={{0,2},{1,3},{2,0},{3,1},{4,6},{5,7},{6,4},{7,5},{8,10},{9,11},{10,... | collective-permute-start | bytes 368648 | tf_op jit(solution)/shard_map/ppermute | solution.py:634
  132.1 14.0 %collective-permute-start.45 = (bf16[160,384]{1,0:T(8,128)(2,1)S(1)}, bf16[160,384]{1,0:T(8,128)(2,1)S(1)}, u32[]{:S(2)}, u32[]{:S(2)}) collective-permute-start(bf16[160,384]{1,0:T(8,128)(2,1)S(1)} %shard_map.325.own), channel_id=1, source_target_pairs={{0,3},{1,2},{2,1},{3,0},{4,7},{5,6},{6,5},{7,4},{8,11},{9,10},{10,... | collective-permute-start | bytes 368648 | tf_op jit(solution)/shard_map/ppermute | solution.py:634
  134.8 13.2 %collective-permute-start.20 = (bf16[256,384]{1,0:T(8,128)(2,1)S(1)}, bf16[256,384]{1,0:T(8,128)(2,1)S(1)}, u32[]{:S(2)}, u32[]{:S(2)}) collective-permute-start(bf16[256,384]{1,0:T(8,128)(2,1)S(1)} %get-tuple-element.186), channel_id=1, source_target_pairs={{0,0},{1,1},{2,6},{3,7},{4,2},{5,3},{6,4},{7,5},{8,8},{9,9},{10,14... | collective-permute-start | bytes 589832 | tf_op jit(solution)/shard_map/ppermute | solution.py:655
  135.5 16.4 %collective-permute-start.21 = (bf16[256,384]{1,0:T(8,128)(2,1)S(1)}, bf16[256,384]{1,0:T(8,128)(2,1)S(1)}, u32[]{:S(2)}, u32[]{:S(2)}) collective-permute-start(bf16[256,384]{1,0:T(8,128)(2,1)S(1)} %get-tuple-element.187), channel_id=1, source_target_pairs={{0,3},{1,0},{2,5},{3,6},{4,1},{5,2},{6,7},{7,4},{8,11},{9,8},{10,1... | collective-permute-start | bytes 589832 | tf_op jit(solution)/shard_map/ppermute | solution.py:655
  145.1 17.1 %collective-permute-start.28 = (bf16[4,128,384]{2,1,0:T(8,128)(2,1)}, bf16[4,128,384]{2,1,0:T(8,128)(2,1)S(1)}, u32[]{:S(2)}, u32[]{:S(2)}) collective-permute-start(bf16[4,128,384]{2,1,0:T(8,128)(2,1)} %get-tuple-element.104), channel_id=1, source_target_pairs={{0,16},{4,20},{8,24},{12,28},{16,0},{20,4},{24,8},{28,12},{1,17},{... | collective-permute-start | bytes 1179656 | tf_op jit(solution)/shard_map/ppermute | solution.py:630
  146.1 16.1 %collective-permute-start.29 = (bf16[4,128,384]{2,1,0:T(8,128)(2,1)S(1)}, bf16[4,128,384]{2,1,0:T(8,128)(2,1)S(1)}, u32[]{:S(2)}, u32[]{:S(2)}) collective-permute-start(bf16[4,128,384]{2,1,0:T(8,128)(2,1)S(1)} %get-tuple-element.105), channel_id=1, source_target_pairs={{0,24},{4,28},{8,16},{12,20},{16,8},{20,12},{24,0},{28,4},{1,25},{... | collective-permute-start | bytes 1179656 | tf_op jit(solution)/shard_map/ppermute | solution.py:630
  148.0 41.1 %collective-permute-start.24 = (f32[512,384]{1,0:T(8,128)S(1)}, f32[512,384]{1,0:T(8,128)S(1)}, u32[]{:S(2)}, u32[]{:S(2)}) collective-permute-start(f32[512,384]{1,0:T(8,128)S(1)} %copy-done.27), channel_id=1, source_target_pairs={{0,4},{4,0},{8,12},{12,8},{16,20},{20,16},{24,28},{28,24},{1,5},{5... | collective-permute-start | bytes 2359304 | tf_op jit(solution)/shard_map/ppermute | solution.py:630
  152.0 13.2 %collective-permute-start.49 = (bf16[160,384]{1,0:T(8,128)(2,1)S(1)}, bf16[160,384]{1,0:T(8,128)(2,1)S(1)}, u32[]{:S(2)}, u32[]{:S(2)}) collective-permute-start(bf16[160,384]{1,0:T(8,128)(2,1)S(1)} %shard_map.326.q0), channel_id=1, source_target_pairs={{0,4},{4,0},{8,12},{12,8},{16,20},{20,16},{24,28},{28,24},{1,5},{5... | collective-permute-start | bytes 368648 | tf_op jit(solution)/shard_map/ppermute | solution.py:630
  152.1 14.7 %collective-permute-start.46 = (bf16[160,384]{1,0:T(8,128)(2,1)S(1)}, bf16[160,384]{1,0:T(8,128)(2,1)S(1)}, u32[]{:S(2)}, u32[]{:S(2)}) collective-permute-start(bf16[160,384]{1,0:T(8,128)(2,1)S(1)} %shard_map.326.q0), channel_id=1, source_target_pairs={{0,8},{4,12},{8,0},{12,4},{16,24},{20,28},{24,16},{28,20},{1,9},{5... | collective-permute-start | bytes 368648 | tf_op jit(solution)/shard_map/ppermute | solution.py:630
  164.4 12.9 %collective-permute-start.47 = (bf16[160,384]{1,0:T(8,128)(2,1)S(1)}, bf16[160,384]{1,0:T(8,128)(2,1)S(1)}, u32[]{:S(2)}, u32[]{:S(2)}) collective-permute-start(bf16[160,384]{1,0:T(8,128)(2,1)S(1)} %shard_map.326.q0), channel_id=1, source_target_pairs={{0,16},{4,20},{8,24},{12,28},{16,0},{20,4},{24,8},{28,12},{1,17},{... | collective-permute-start | bytes 368648 | tf_op jit(solution)/shard_map/ppermute | solution.py:630
  165.2 13.2 %collective-permute-start.48 = (bf16[160,384]{1,0:T(8,128)(2,1)S(1)}, bf16[160,384]{1,0:T(8,128)(2,1)S(1)}, u32[]{:S(2)}, u32[]{:S(2)}) collective-permute-start(bf16[160,384]{1,0:T(8,128)(2,1)S(1)} %shard_map.326.q0), channel_id=1, source_target_pairs={{0,24},{4,28},{8,16},{12,20},{16,8},{20,12},{24,0},{28,4},{1,25},{... | collective-permute-start | bytes 368648 | tf_op jit(solution)/shard_map/ppermute | solution.py:630
  175.5 13.2 %collective-permute-start.50 = (bf16[160,384]{1,0:T(8,128)(2,1)S(1)}, bf16[160,384]{1,0:T(8,128)(2,1)S(1)}, u32[]{:S(2)}, u32[]{:S(2)}) collective-permute-start(bf16[160,384]{1,0:T(8,128)(2,1)S(1)} %collective-permute-done.46.q1), channel_id=1, source_target_pairs={{0,4},{4,0},{8,12},{12,8},{16,20},{20,16},{24,28},{28,24},{1,5},{5... | collective-permute-start | bytes 368648 | tf_op jit(solution)/shard_map/ppermute | solution.py:630
  181.9 12.2 %collective-permute-start.51 = (bf16[160,384]{1,0:T(8,128)(2,1)S(1)}, bf16[160,384]{1,0:T(8,128)(2,1)S(1)}, u32[]{:S(2)}, u32[]{:S(2)}) collective-permute-start(bf16[160,384]{1,0:T(8,128)(2,1)S(1)} %collective-permute-done.47.q2), channel_id=1, source_target_pairs={{0,4},{4,0},{8,12},{12,8},{16,20},{20,16},{24,28},{28,24},{1,5},{5... | collective-permute-start | bytes 368648 | tf_op jit(solution)/shard_map/ppermute | solution.py:630
  187.3 14.8 %collective-permute-start.36 = (bf16[4,128,384]{2,1,0:T(8,128)(2,1)S(1)}, bf16[4,128,384]{2,1,0:T(8,128)(2,1)S(1)}, u32[]{:S(2)}, u32[]{:S(2)}) collective-permute-start(bf16[4,128,384]{2,1,0:T(8,128)(2,1)S(1)} %pad_maximum_fusion.2.a0), channel_id=1, source_target_pairs={{0,8},{4,12},{8,0},{12,4},{16,24},{20,28},{24,16},{28,20},{1,9},{5... | collective-permute-start | bytes 1179656 | tf_op jit(solution)/shard_map/ppermute | solution.py:630
  188.8 17.9 %collective-permute-start.37 = (bf16[4,128,384]{2,1,0:T(8,128)(2,1)S(1)}, bf16[4,128,384]{2,1,0:T(8,128)(2,1)S(1)}, u32[]{:S(2)}, u32[]{:S(2)}) collective-permute-start(bf16[4,128,384]{2,1,0:T(8,128)(2,1)S(1)} %pad_maximum_fusion.2.a0), channel_id=1, source_target_pairs={{0,16},{4,20},{8,24},{12,28},{16,0},{20,4},{24,8},{28,12},{1,17},{... | collective-permute-start | bytes 1179656 | tf_op jit(solution)/shard_map/ppermute | solution.py:630
  189.2 19.3 %collective-permute-start.38 = (bf16[4,128,384]{2,1,0:T(8,128)(2,1)S(1)}, bf16[4,128,384]{2,1,0:T(8,128)(2,1)S(1)}, u32[]{:S(2)}, u32[]{:S(2)}) collective-permute-start(bf16[4,128,384]{2,1,0:T(8,128)(2,1)S(1)} %pad_maximum_fusion.2.a0), channel_id=1, source_target_pairs={{0,24},{4,28},{8,16},{12,20},{16,8},{20,12},{24,0},{28,4},{1,25},{... | collective-permute-start | bytes 1179656 | tf_op jit(solution)/shard_map/ppermute | solution.py:630
  194.1 48.2 %collective-permute-start.25 = (f32[256,384]{1,0:T(8,128)}, f32[256,384]{1,0:T(8,128)}, u32[]{:S(2)}, u32[]{:S(2)}) collective-permute-start(f32[256,384]{1,0:T(8,128)} %get-tuple-element.100), channel_id=1, source_target_pairs={{0,0},{1,1},{2,6},{3,7},{4,2},{5,3},{6,4},{7,5},{8,8},{9,9},{10,14... | collective-permute-start | bytes 1179656 | tf_op jit(solution)/shard_map/ppermute | solution.py:655
  198.6 43.7 %collective-permute-start.26 = (f32[256,384]{1,0:T(8,128)}, f32[256,384]{1,0:T(8,128)}, u32[]{:S(2)}, u32[]{:S(2)}) collective-permute-start(f32[256,384]{1,0:T(8,128)} %get-tuple-element.101), channel_id=1, source_target_pairs={{0,3},{1,0},{2,5},{3,6},{4,1},{5,2},{6,7},{7,4},{8,11},{9,8},{10,1... | collective-permute-start | bytes 1179656 | tf_op jit(solution)/shard_map/ppermute | solution.py:655
  223.9 20.6 %collective-permute-start.53 = (f32[384,384]{1,0:T(8,128)}, f32[384,384]{1,0:T(8,128)S(1)}, u32[]{:S(2)}, u32[]{:S(2)}) collective-permute-start(f32[384,384]{1,0:T(8,128)} %shard_map.327.two), channel_id=1, source_target_pairs={{0,4},{4,0},{8,12},{12,8},{16,20},{20,16},{24,28},{28,24},{1,5},{5... | collective-permute-start | bytes 1769480 | tf_op jit(solution)/shard_map/ppermute | solution.py:630
  (51 other events, 668.8 us)
